TPU v7x, 128 devices: a whole 4x4x4 slice. The times are simulated.
128 devices in a mesh: slab: 32 (over z, x, core), bal: 4 (over y).
Axes of the slice: x: 4, y: 4, z: 4, core: 2. Of those that a mesh axis runs over, the one named last changes fastest.
Arguments:
- volume: bfloat16 [128, 4, 64, 4096], P(('slab', 'bal')), may hold values from -150 to 150
- first_kernel: bfloat16 [3, 3, 3, 32], replicated, may hold values from -1.25 to 1.25
- second_kernel: bfloat16 [3, 3, 3, 32, 32], replicated, may hold values from -0.21875 to 0.21875
- class_weights: bfloat16 [32, 3], replicated, may hold values from -40 to 40
- patch_corners: int32 [128, 6, 3], P(('slab', 'bal')), may hold values from 0 to 127, as said below
- patch_counts: int32 [128], replicated, may hold values from 0 to 6, as said below
Outputs:
- probabilities: float32 [128, 4, 64, 3, 4096], P(('slab', 'bal'))
Inputs may be any that keep to these rules, and one draw needn't show every extreme that they name: `patch_corners`: entry x of every corner equals its column's index; for tissue patches x + 1 < 128; y <= 2 and z <= 62. The entries of one column's list are different corners; entries past patch_counts are listed corners that are not tissue patches. `patch_counts`: the last column has none; every other column has at least one. In every group of 4 consecutive columns one column has exactly 6; the columns of a group hold at most 12 together, and some group exactly that many.
All inputs are finite; a program needn't handle non-finite values.
Results may differ from a plain program's by a relative error of at most 0.0086.
Values may be sent and summed in bfloat16 or wider, within the bound.
No kernel may reach another device: no remote copies, remote signals or barrier semaphores. Data moves between devices by JAX's collectives and lax.ppermute only.
A program may use at most 128 MiB of HBM per device.

v0:
```python
import jax
import jax.numpy as jnp
import numpy as np
from jax import lax
from jax.experimental import pallas as pl
from jax.experimental.pallas import tpu as pltpu
from jax.sharding import PartitionSpec as P

PATCH = 32
HALF = 16
TILE_VOX = 4096
CHANNELS = 32
CLASSES = 3
ENTRIES = 7
SENT = 2
HOME_MOST = 6
TILES_Y = 4
TILES_Z = 64
F32 = jnp.float32
BF16 = jnp.bfloat16
MIB = 1024 * 1024


def select_x():
    out = np.zeros((4, 16, 32), np.float32)
    for wx in range(4):
        for bx in range(16):
            x = 2 * bx - 1 + wx
            if 0 <= x < 32:
                out[wx, bx, x] = 1
    return out.reshape(64, 32)


def select_window():
    out = np.zeros((4, 2, 2, 16, 3, 4, 2, 16), np.float32)
    for wx in range(4):
        for ypar in range(2):
            for g in range(3):
                for zw in range(16):
                    z = 12 * g - 2 + zw
                    if 0 <= z < 32:
                        out[wx, z // 16, ypar, z % 16, g, wx, ypar, zw] = 1
    return out.reshape(256, 384)


def blend_map():
    coordinate = np.arange(PATCH, dtype=np.float32)
    square = (coordinate - np.float32(15.5)) ** 2 / np.float32(32.0)
    total = square[:, None, None] + square[None, :, None] + square[None, None, :]
    return (np.float32(0.1) + np.float32(0.9) * np.exp(-total)).astype(np.float32)


def blend_rows():
    b = blend_map().reshape(16, 2, 16, 2, 2, 16)
    return b.transpose(2, 0, 4, 1, 3, 5).reshape(256, 128)


def blend_parts():
    b = blend_map().reshape(2, 16, 2, 16, 2, 16).transpose(0, 2, 4, 1, 3, 5).reshape(2, 4, TILE_VOX)
    out = np.zeros((4, 64, TILE_VOX), np.float32)
    for side in range(2):
        for patch in range(ENTRIES):
            at = 4 * (ENTRIES * side + patch)
            rest = b[side]
            for part in range(3):
                top = rest.astype(jnp.bfloat16).astype(np.float32)
                out[part, at : at + 4] = top
                rest = rest - top
    return out.reshape(256, TILE_VOX)


def call(kernel, vmem, **options):
    params = pltpu.CompilerParams(vmem_limit_bytes=vmem * MIB)
    return pl.pallas_call(kernel, compiler_params=params, **options)


SMEM_SPEC = pl.BlockSpec(memory_space=pltpu.SMEM)
VMEM_SPEC = pl.BlockSpec(memory_space=pltpu.VMEM)


def write_plan(column_ref, count_ref, plan_ref, sent):
    column = column_ref[0]

    def group_plan(group, at):
        heavy = jnp.int32(0)
        for i in (3, 2, 1, 0):
            heavy = jnp.where(count_ref[4 * group + i] == HOME_MOST, i, heavy)
        place = [(heavy + k) % 4 for k in range(4)]
        count = [count_ref[4 * group + place[k]] for k in range(4)]
        left = [jnp.where((count[1] >= 4) & (heavy >= 1), 1, 0), 0, 0, 0]
        right = []
        coming = 0
        for k in range(4):
            load = count[k] + coming - left[k]
            if k == 3:
                load = load + left[0]
                left[3] = jnp.where((load > 3) & (place[3] >= 1), 1, 0)
                load = load - left[3]
            out = jnp.clip(load - 3, 0, jnp.minimum(count[k] - left[k], 3))
            right.append(out)
            coming = out
        for k in range(4):
            sent[at + place[k]] = right[k]
            sent[at + 4 + place[k]] = left[k]

    def column_plan(where, at, out):
        me = where % 4
        right, left = sent[at + me], sent[at + 4 + me]
        plan_ref[out] = count_ref[where] - right - left
        plan_ref[out + 1] = right
        plan_ref[out + 2] = left

    group_plan(column // 4, 0)
    column_plan(column, 0, 0)
    me = column % 4
    plan_ref[6] = sent[(me + 3) % 4]
    plan_ref[7] = jnp.where(me == 3, 0, sent[4 + (me + 1) % 4])
    plan_ref[8] = jnp.where(me == 0, 1, 0)
    before = jnp.maximum(column - 1, 0)
    group_plan(before // 4, 8)
    column_plan(before, 8, 3)

    @pl.when(column == 0)
    def _():
        for i in range(3):
            plan_ref[3 + i] = 0


def flatten(volume_ref, copies, flat):
    for ty in range(TILES_Y):
        copies[ty].wait()
        for group in range(TILES_Z // 16):
            for lane_tile in range(32):
                block = volume_ref[ty, 16 * group : 16 * group + 16, 128 * lane_tile : 128 * lane_tile + 128].astype(F32)
                for half in range(2):
                    start = ((ty * 8 + 2 * group + half) * 32 + lane_tile) * 8
                    flat[start : start + 8, :] = block[8 * half : 8 * half + 8]


def take_tiles(corner_ref, flat, out_ref, slot, place):
    for tile in range(4):
        ty = corner_ref[1, 0, slot] + tile // 2
        tz = corner_ref[2, 0, slot] + tile % 2
        base = (ty * 8 + tz // 8) * 256 + tz % 8
        rows = []
        for x_half in range(2):
            parts = [flat[pl.ds(base + 128 * x_half + 8 * h, 8, stride=16), :] for h in range(2)]
            rows.append(jnp.concatenate(parts, axis=1))
        out_ref[place, tile] = jnp.concatenate(rows, axis=0).astype(BF16)


def take_entries(plan_ref, at, corner_ref, flat, kept_out, right_out, left_out):
    kept, right = plan_ref[at], plan_ref[at + 1]

    @pl.loop(0, kept)
    def _(slot):
        take_tiles(corner_ref, flat, kept_out, slot, slot)

    @pl.loop(0, right)
    def _(slot):
        take_tiles(corner_ref, flat, right_out, kept + slot, slot)

    @pl.when(plan_ref[at + 2] == 1)
    def _():
        take_tiles(corner_ref, flat, left_out, kept + right, 0)


def gather_kernel(
    column_ref, prev_ref, count_hbm, own_hbm, volume_hbm,
    plan_ref, kept_out, right_out, back_out, here_out, two_back_out,
    flat, own_left, sent, count_ref, own_ref, volume_ref, arrived,
):
    count_copy = pltpu.make_async_copy(count_hbm, count_ref, arrived.at[4])
    own_copy = pltpu.make_async_copy(own_hbm, own_ref, arrived.at[5])
    copies = [pltpu.make_async_copy(volume_hbm.at[ty], volume_ref.at[ty], arrived.at[ty]) for ty in range(TILES_Y)]
    for copy in [count_copy, own_copy] + copies:
        copy.start()
    count_copy.wait()
    write_plan(column_ref, count_ref, plan_ref, sent)
    own_copy.wait()
    flatten(volume_ref, copies, flat)
    take_entries(plan_ref, 0, own_ref, flat, kept_out, right_out, own_left)
    take_entries(plan_ref, 3, prev_ref, flat, back_out, here_out, two_back_out)
    back_out[3] = own_left[0]


def gather(column, patch_counts, corners, prev_corners, volume):
    def tiles(count):
        return jax.ShapeDtypeStruct((count, 4, 16, 256), BF16)

    return call(
        gather_kernel,
        58,
        out_shape=(jax.ShapeDtypeStruct((9,), jnp.int32), tiles(3), tiles(3), tiles(4), tiles(3), tiles(1)),
        in_specs=[SMEM_SPEC] * 2 + [pl.BlockSpec(memory_space=pltpu.HBM)] * 3,
        out_specs=(SMEM_SPEC,) + (VMEM_SPEC,) * 5,
        scratch_shapes=[
            pltpu.VMEM((TILES_Y * TILES_Z * 32, 128), F32),
            pltpu.VMEM((1, 4, 16, 256), BF16),
            pltpu.SMEM((16,), jnp.int32),
            pltpu.SMEM(patch_counts.shape, jnp.int32),
            pltpu.SMEM(corners.shape, jnp.int32),
            pltpu.VMEM((TILES_Y, TILES_Z, TILE_VOX), BF16),
            pltpu.SemaphoreType.DMA((6,)),
        ],
        name="gather",
    )(column, prev_corners, patch_counts, corners, volume)


def dot(a, b):
    return jnp.dot(a, b, preferred_element_type=F32)


def weights_kernel(first_ref, second_ref, class_ref, first_out, second_out, class_out, four, taps, turned):
    lane = lax.broadcasted_iota(jnp.int32, (32, 256), 1)
    taps[...] = jnp.zeros((32, 32), F32)
    for dx in range(3):
        for dy in range(3):
            at = 9 * dx + 3 * dy
            taps[at : at + 3, :] = first_ref[dx, dy].astype(F32)
    first = jnp.concatenate([taps[...]] * 8, axis=1)
    big = jnp.concatenate([jnp.where(lane // 32 == s, first, 0.0).astype(BF16) for s in range(8)], axis=0)
    row = lax.broadcasted_iota(jnp.int32, (256, 256), 0)
    col = lax.broadcasted_iota(jnp.int32, (256, 256), 1)
    tap = col % 32
    dx = jnp.where(tap >= 18, 2, jnp.where(tap >= 9, 1, 0))
    rest = tap - 9 * dx
    dy = jnp.where(rest >= 6, 2, jnp.where(rest >= 3, 1, 0))
    dz = rest - 3 * dy
    fits = ((row // 32) % 4 == col // 128 + dx) & (row // 128 * 2 + (row // 16) % 2 == (col // 64) % 2 + dy) & (tap < 27)
    ahead = row % 16 - (col // 32) % 2 - dz
    for j in range(6):
        spread = jnp.where(fits & (ahead == 2 * j), 1.0, 0.0).astype(BF16)
        first_out[j] = dot(spread, big).astype(BF16)

    part = lax.broadcasted_iota(jnp.int32, (32, 128), 1) // 32
    for tap in range(27):
        four[tap] = jnp.concatenate([second_ref[tap].astype(F32)] * 4, axis=1)
    for qx in range(4):
        for qy in range(4):
            for qz in range(4):
                at = ((((qy // 2 * 2 + qz // 2) * 2 + qx // 2) * 2 + qx % 2) * 2 + qy % 2) * 2 + qz % 2
                for half in range(2):
                    got = jnp.zeros((32, 128), F32)
                    for s in range(4):
                        dx, dy, dz = qx - half, qy - s // 2, qz - s % 2
                        if min(dx, dy, dz) >= 0 and max(dx, dy, dz) <= 2:
                            got = jnp.where(part == s, four[(dx * 3 + dy) * 3 + dz], got)
                    second_out[32 * at : 32 * at + 32, 128 * half : 128 * half + 128] = got.astype(BF16)

    turned[...] = jnp.zeros((128, 128), F32)
    turned[0:CLASSES, 0:CHANNELS] = class_ref[...].astype(F32)
    classes = turned[...].T
    columns = jnp.zeros((32, 256), F32)
    for k in range(CLASSES):
        columns = jnp.where(lane // 64 == k, classes[0:32, k : k + 1], columns)
    for b in range(8):
        for s in range(8):
            place = 32 * (s // 4) + 16 * (s // 2 % 2) + 2 * b + s % 2
            class_out[b, 32 * s : 32 * s + 32, :] = jnp.where(lane % 64 == place, columns, 0.0).astype(BF16)


def prepare_weights(first_kernel, second_kernel, class_weights):
    return call(
        weights_kernel,
        12,
        out_shape=(
            jax.ShapeDtypeStruct((6, 256, 256), BF16),
            jax.ShapeDtypeStruct((2048, 256), BF16),
            jax.ShapeDtypeStruct((8, 256, 256), BF16),
        ),
        in_specs=[VMEM_SPEC] * 3,
        out_specs=(VMEM_SPEC,) * 3,
        scratch_shapes=[pltpu.VMEM((27, 32, 128), F32), pltpu.VMEM((32, 32), F32), pltpu.VMEM((128, 128), F32)],
        cost_estimate=pl.CostEstimate(flops=1_000_000_000, bytes_accessed=8_000_000, transcendentals=0),
        name="weights",
    )(first_kernel, second_kernel.reshape(27, CHANNELS, CHANNELS), class_weights.T)


def fold_channels(row):
    half = row[:, :128] + row[:, 128:]
    half = half + pltpu.roll(half, 64, 1)
    half = half + pltpu.roll(half, 32, 1)
    return jnp.concatenate([half, half], axis=1)


def merge_stats(pivot, s1, s2):
    count = 4096.0
    lane_mean = pivot + s1 * (1.0 / count)
    lane_m2 = s2 - s1 * s1 * (1.0 / count)
    mean = fold_channels(lane_mean) * 0.125
    off = lane_mean - mean
    var = fold_channels(lane_m2 + count * (off * off)) * (1.0 / 32768.0)
    return mean, lax.rsqrt(var + 1e-05)


def leaky(v):
    return jnp.maximum(v, 0.01 * v)


def sum_rows(block):
    return jnp.sum(block, axis=0, keepdims=True)


def network_kernel(plan_ref, own_ref, back_ref, right_ref, here_ref, across_ref, left_ref, *refs):
    pick_ref, window_ref, first_ref, second_ref, class_ref, blend_ref = refs[:6]
    outs, (cubes, made, spread, raw, hidden_a, hidden_b, second) = refs[6:-7], refs[-7:]
    for i in range(3):
        cubes[i, 0] = own_ref[i]
        cubes[i, 1] = back_ref[i]
        cubes[3 + i, 0] = right_ref[i]
    cubes[6, 0] = back_ref[3]
    cubes[6, 1] = left_ref[0]

    @pl.when(plan_ref[8] == 0)
    def _():
        for i in range(3):
            cubes[3 + i, 1] = here_ref[i]

    @pl.when(plan_ref[8] == 1)
    def _():
        for i in range(3):
            cubes[3 + i, 1] = across_ref[i]

    spread[0] = jnp.zeros((16, 384), BF16)
    spread[17] = jnp.zeros((16, 384), BF16)
    lane = lax.broadcasted_iota(jnp.int32, (1, 256), 1)
    sy, sz = (lane % 128) // 64, (lane % 64) // 32
    y_first = (sy == 1).astype(F32)
    y_last = (sy == 0).astype(F32)
    row16 = lax.broadcasted_iota(jnp.int32, (16, 128), 0)
    lane16 = lax.broadcasted_iota(jnp.int32, (16, 128), 1) // 32

    def z_mask(bz):
        bad = ((bz == 0) & (sz == 0)) | ((bz == 16) & (sz == 1))
        return jnp.where(bad, 0.0, 1.0)

    def patch(index, carry):
        kept = plan_ref[0]
        later = jnp.where(index - kept < plan_ref[6], 3 + index - kept, 6)
        slot = jnp.where(index < kept, index, later)
        cube = jnp.concatenate(
            [jnp.concatenate([cubes[slot, tx, t] for t in range(4)], axis=1) for tx in range(2)], axis=0
        )
        moved = dot(pick_ref[...], cube)
        lists = []
        for ty in range(2):
            for quad in range(2):
                pieces = []
                for wx in range(4):
                    for tz in range(2):
                        at = (ty * 2 + tz) * 256 + quad * 128
                        pieces.append(moved[16 * wx : 16 * wx + 16, at : at + 128])
                for r in range(4):
                    joined = []
                    for tile in range(2):
                        got = None
                        for place in range(4):
                            piece = pieces[4 * tile + place]
                            turn = (32 * (place - r)) % 128
                            if turn:
                                piece = pltpu.roll(piece, turn, 1)
                            got = piece if got is None else jnp.where(lane16 == place, piece, got)
                        joined.append(got)
                    lists.append(jnp.concatenate(joined, axis=1).astype(BF16))
        rows = jnp.concatenate(lists, axis=0)
        spread[1:17] = dot(rows, window_ref[...]).astype(BF16).reshape(16, 16, 384)

        def first_plane(bz):
            lanes = slice(128 * (bz // 6), 128 * (bz // 6) + 128)
            lhs = jnp.concatenate([spread[0:17, :, lanes], spread[1:18, :, lanes]], axis=2).reshape(272, 256)
            out = dot(lhs, first_ref[bz % 6])
            raw[bz] = out
            return out

        def plane_sums(bz, out, pivot):
            d = out - pivot
            inner = d[16:256].reshape(15, 16, 256)
            edges = d[0:16] * y_first, d[256:272] * y_last
            s1 = jnp.sum(inner, axis=0) + (edges[0] + edges[1])
            s2 = jnp.sum(inner * inner, axis=0) + (edges[0] * edges[0] + edges[1] * edges[1])
            if bz in (0, 16):
                s1, s2 = s1 * z_mask(bz), s2 * z_mask(bz)
            return s1, s2

        out = first_plane(1)
        pivot = sum_rows(out[16:256]) * (1.0 / 240.0)
        s1, s2 = plane_sums(1, out, pivot)
        for bz in range(17):
            if bz != 1:
                a1, a2 = plane_sums(bz, first_plane(bz), pivot)
                s1, s2 = s1 + a1, s2 + a2
        mean, inv = merge_stats(pivot, sum_rows(s1), sum_rows(s2))

        def normalise(bz, into, place):
            scale = inv * z_mask(bz)
            for by in range(17):
                here = scale * y_first if by == 0 else scale * y_last if by == 16 else scale
                v = leaky((raw[bz, 16 * by : 16 * by + 16] - mean) * here)
                even, odd = v[:, :128], v[:, 128:]
                before = jnp.where(row16 == 0, 0.0, pltpu.roll(odd, 1, 0))
                after = jnp.where(row16 == 15, 0.0, pltpu.roll(even, 15, 0))
                into[place, by] = jnp.concatenate([before, even, odd, after], axis=1).astype(BF16)

        def second_rows(held, first, rows):
            parts = [held[first + ez, ey : ey + rows].reshape(16 * rows, 512) for ey in range(2) for ez in range(2)]
            return jnp.concatenate(parts, axis=1)

        def second_four(four, held, pivot):
            lhs = jnp.concatenate([second_rows(held, i, 16) for i in range(4)], axis=0)
            slabs = dot(lhs, second_ref[...])
            second[pl.ds(4 * four, 4)] = slabs.reshape(4, 256, 256)
            d = (slabs - pivot).reshape(64, 16, 256)
            return jnp.sum(d, axis=0), jnp.sum(d * d, axis=0)

        for bz in range(5):
            normalise(bz, hidden_a, bz)
        pivot2 = sum_rows(dot(second_rows(hidden_a, 0, 8), second_ref[...])) * (1.0 / 128.0)

        def second_loop(i, sums):
            s1, s2 = sums
            for half, (held, later) in enumerate(((hidden_a, hidden_b), (hidden_b, hidden_a))):
                a1, a2 = second_four(2 * i + half, held, pivot2)
                later[0] = held[4]
                for ahead in range(4):
                    normalise(jnp.minimum(8 * i + 4 * half + 5 + ahead, 16), later, 1 + ahead)
                s1, s2 = s1 + a1, s2 + a2
            return s1, s2

        zeros = jnp.zeros((16, 256), F32)
        s1, s2 = lax.fori_loop(0, 2, second_loop, (zeros, zeros))
        mean, inv = merge_stats(pivot2, sum_rows(s1), sum_rows(s2))

        logits = []
        for tz in range(2):
            parts, weights = [], []
            for b in range(8):
                h = leaky((second[8 * tz + b] - mean) * inv)
                top = h.astype(BF16)
                parts += [top, (h - top.astype(F32)).astype(BF16)]
                weights += [class_ref[b], class_ref[b]]
            logits.append(dot(jnp.concatenate(parts, axis=1), jnp.concatenate(weights, axis=0)))

        side = lax.broadcasted_iota(jnp.int32, (256, 128), 1) < 64
        t0, t1 = logits[0][:, 0:128], logits[0][:, 128:256]
        u0, u1 = logits[1][:, 0:128], logits[1][:, 128:256]
        l0 = jnp.where(side, t0, pltpu.roll(u0, 64, 1))
        l1 = jnp.where(side, pltpu.roll(t0, 64, 1), u0)
        l2 = jnp.where(side, t1, pltpu.roll(u1, 64, 1))
        most = jnp.maximum(jnp.maximum(l0, l1), l2)
        x0, x1, x2 = jnp.exp(l0 - most), jnp.exp(l1 - most), jnp.exp(l2 - most)
        share = blend_ref[...] / (x0 + x1 + x2)

        lane32 = lax.broadcasted_iota(jnp.int32, (64, 128), 1) // 32
        for k, x in enumerate((x0, x1)):
            w = (x * share).reshape(4, 4, 16, 128)
            sources = [w[:, r].reshape(64, 128) for r in range(4)]
            dest = []
            for q in range(4):
                got = None
                for r in range(4):
                    turn = (32 * (r - q)) % 128
                    piece = pltpu.roll(sources[r], turn, 1) if turn else sources[r]
                    got = piece if got is None else jnp.where(lane32 == r, piece, got)
                dest.append(got)
            for tx in range(2):
                for ty in range(2):
                    for h in range(2):
                        at = (2 * ty + h) * 16 + 8 * tx
                        for tz in range(2):
                            both = jnp.concatenate([dest[2 * tz][at : at + 8], dest[2 * tz + 1][at : at + 8]], axis=0)
                            rows = slice(16 * k, 16 * k + 16)
                            lanes = slice(128 * h, 128 * h + 128)
                            made[tx, slot, 2 * ty + tz, rows, lanes] = both.astype(BF16)
        return carry

    lax.fori_loop(0, plan_ref[0] + plan_ref[6] + plan_ref[7], patch, 0)
    low_out, ahead_out, right_low_out, right_up_out, left_up_out = outs
    low_out[...] = made[0, 0:3]
    ahead_out[0:3] = made[1, 0:3]
    ahead_out[3] = made[0, 6]
    right_low_out[...] = made[0, 3:6]
    right_up_out[...] = made[1, 3:6]
    left_up_out[0] = made[1, 6]


def network(plan, cubes, weights):
    def halves(count):
        return jax.ShapeDtypeStruct((count, 4, 16 * SENT, 256), BF16)

    return call(
        network_kernel,
        32,
        out_shape=(halves(3), halves(4), halves(3), halves(3), halves(1)),
        in_specs=[SMEM_SPEC] + [VMEM_SPEC] * 12,
        out_specs=(VMEM_SPEC,) * 5,
        scratch_shapes=[
            pltpu.VMEM((ENTRIES, 2, 4, 16, 256), BF16),
            pltpu.VMEM((2, ENTRIES, 4, 16 * SENT, 256), BF16),
            pltpu.VMEM((18, 16, 384), BF16),
            pltpu.VMEM((17, 272, 256), F32),
            pltpu.VMEM((5, 17, 16, 512), BF16),
            pltpu.VMEM((5, 17, 16, 512), BF16),
            pltpu.VMEM((16, 256, 256), F32),
        ],
        cost_estimate=pl.CostEstimate(flops=20_000_000_000, bytes_accessed=8_000_000, transcendentals=600_000),
        name="network",
    )(plan, *cubes, *weights)


def patch_entry(plan_ref, side, i):
    kept, right, left = [plan_ref[3 * side + j] for j in range(3)]
    if i < 3:
        return i < kept, jnp.int32(i)
    if i < 6:
        return i - 3 < right, jnp.minimum(kept + i - 3, HOME_MOST - 1)
    return left == 1, jnp.minimum(kept + right, HOME_MOST - 1)


def inverse_kernel(plan_ref, own_ref, prev_ref, parts_ref, inverse_ref, chosen_ref, chosen_parts):
    @pl.when(pl.program_id(0) == 0)
    def _():
        lane = lax.broadcasted_iota(jnp.int32, (1, 256), 1) % 64
        tiles = jnp.full((1, 256), -1, jnp.int32)
        for side, corner_ref in enumerate((own_ref, prev_ref)):
            for i in range(ENTRIES):
                live, slot = patch_entry(plan_ref, side, i)
                first = corner_ref[1, 0, slot] * TILES_Z + corner_ref[2, 0, slot]
                for t in range(4):
                    tile = jnp.where(live, first + TILES_Z * (t // 2) + t % 2, -1)
                    tiles = jnp.where(lane == 4 * (ENTRIES * side + i) + t, tile, tiles)
        same = lax.broadcasted_iota(jnp.int32, (256, 256), 0) == tiles
        hot = jnp.where(same, 1.0, 0.0).astype(BF16)
        chosen_parts[...] = hot
        chosen_ref[...] = hot[:, :128]

    weight = dot(chosen_parts[...], parts_ref[...])
    inverse_ref[...] = jnp.where(weight > 0, 1.0 / jnp.maximum(weight, 0.1), 0.0)


def inverse_weights(plan, corners, prev_corners):
    return call(
        inverse_kernel,
        12,
        grid=(4,),
        out_shape=(
            jax.ShapeDtypeStruct((TILES_Y * TILES_Z, TILE_VOX), F32),
            jax.ShapeDtypeStruct((TILES_Y * TILES_Z, 128), BF16),
        ),
        in_specs=[SMEM_SPEC] * 3 + [pl.BlockSpec((256, 1024), lambda i: (0, i))],
        out_specs=(pl.BlockSpec((256, 1024), lambda i: (0, i)), pl.BlockSpec((256, 128), lambda i: (0, 0))),
        scratch_shapes=[pltpu.VMEM((256, 256), BF16)],
        cost_estimate=pl.CostEstimate(flops=1_000_000_000, bytes_accessed=8_000_000, transcendentals=0),
        name="inverse_weights",
    )(plan, corners, prev_corners, jnp.asarray(blend_parts(), BF16))


def blend_kernel(
    plan_ref, chosen_ref, inverse_ref, low_ref, right_ref, ahead_ref, here_ref, across_ref, left_ref, out_ref, rows, stacked, staged, written
):
    for side in range(2):
        for i in range(ENTRIES):
            live, _ = patch_entry(plan_ref, side, i)
            number = 4 * (ENTRIES * side + i)
            if i < 3:
                kept_ref = (low_ref, ahead_ref)[side]
                sources = [(live, kept_ref, i)]
            elif i == 6:
                sources = [(live, left_ref, 0) if side else (live, ahead_ref, 3)]
            elif side == 0:
                sources = [(live, right_ref, i - 3)]
            else:
                starts = plan_ref[8] == 1
                sources = [
                    (live & jnp.logical_not(starts), here_ref, i - 3),
                    (live & starts, across_ref, i - 3),
                ]
            for when, part_ref, place in sources:

                @pl.when(when)
                def _():
                    for t in range(4):
                        for h in range(2):
                            piece = part_ref[place, t, :, 128 * h : 128 * h + 128]
                            at = 40 * (number + t)
                            rows[h, at : at + 16 * SENT, :] = piece.astype(F32)

            @pl.when(jnp.logical_not(live))
            def _():
                for h in range(2):
                    rows[h, 40 * number : 40 * number + 160, :] = jnp.zeros((160, 128), F32)

    blank = jnp.zeros((8, 128), F32)
    for x in range(16):
        for k in range(SENT):
            row = 16 * k + (x % 2) * 8 + x // 2
            for h in range(2):
                for pair in range(4):
                    both = [rows[h, pl.ds(640 * pair + 320 * o + row, 8, stride=40), :] if 2 * pair + o < 7 else blank for o in range(2)]
                    at = 256 * k + 128 * h
                    stacked[x, 16 * pair : 16 * pair + 16, at : at + 128] = jnp.concatenate(both, axis=0).astype(BF16)

    def part_copy(x):
        lanes = pl.ds(pl.multiple_of(256 * x, 256), 256)
        return pltpu.make_async_copy(staged.at[:, :, :, lanes], out_ref.at[:, :, :, lanes], written.at[x])

    @pl.loop(0, 16)
    def _(x):
        lanes = pl.ds(pl.multiple_of(256 * x, 256), 256)
        inv = inverse_ref[:, lanes]
        got = dot(chosen_ref[:, 0:64], stacked[x])
        p0, p1 = got[:, :256] * inv, got[:, 256:] * inv
        p2 = jnp.where(inv > 0, jnp.maximum(1.0 - p0 - p1, 0.0), 0.0)
        for k, p in enumerate((p0, p1, p2)):
            staged[:, k, :, lanes] = p.reshape(TILES_Y, TILES_Z, 256)
        part_copy(x).start()

    @pl.loop(0, 16)
    def _(x):
        part_copy(x).wait()


def blend(plan, chosen, inverse, *parts):
    shape = (TILES_Y, CLASSES, TILES_Z, TILE_VOX)
    return call(
        blend_kernel,
        28,
        out_shape=jax.ShapeDtypeStruct(shape, F32),
        in_specs=[SMEM_SPEC] + [VMEM_SPEC] * 8,
        out_specs=pl.BlockSpec(memory_space=pl.ANY),
        scratch_shapes=[
            pltpu.VMEM((2, 8 * ENTRIES * 40, 128), F32),
            pltpu.VMEM((16, 64, 256 * SENT), BF16),
            pltpu.VMEM(shape, F32),
            pltpu.SemaphoreType.DMA((16,)),
        ],
        name="blend",
    )(plan, chosen, inverse, *parts)


def passed_along(block, axis, distance):
    devices = range(lax.axis_size(axis))
    route = [(i - distance, i) for i in devices if i - distance in devices]
    return lax.ppermute(block, axis, route)


def passed_round(block, distance):
    size = lax.axis_size("bal")
    return lax.ppermute(block, "bal", [(i, (i + distance) % size) for i in range(size)])


def passed_over(block, forward):
    axes = ("slab", "bal")
    members = lax.axis_size("bal")
    pairs = [(i, i + members) for i in range(0, lax.axis_size(axes) - members, members)]
    return lax.ppermute(block, axes, pairs if forward else [(b, a) for a, b in pairs])


def local(volume, first_kernel, second_kernel, class_weights, patch_corners, patch_counts):
    axes = ("slab", "bal")
    column = lax.axis_index(axes).astype(jnp.int32)
    corners = patch_corners.transpose(2, 0, 1)
    prev_corners = passed_along(corners, axes, 1)
    plan, own_kept, own_right, back, here, two_back = gather(column[None], patch_counts, corners, prev_corners, volume[0])
    right = passed_round(own_right, 1)
    back = passed_along(back, axes, -1)
    across = passed_over(here, False)
    left = passed_along(two_back, axes, -2)
    weights = (
        jnp.asarray(select_x(), BF16),
        jnp.asarray(select_window(), BF16),
        *prepare_weights(first_kernel, second_kernel, class_weights),
        jnp.asarray(blend_rows(), F32),
    )
    low, ahead, right_low, right_up, left_up = network(plan, (own_kept, back, right, here, across, left), weights)
    ahead = passed_along(ahead, axes, 1)
    right_low = passed_round(right_low, -1)
    across_up = passed_over(right_up, True)
    left_up = passed_along(left_up, axes, 2)
    corners, prev_corners, low = lax.optimization_barrier((corners, prev_corners, low))
    inverse, chosen = inverse_weights(plan, corners, prev_corners)
    out = blend(plan, chosen, inverse, low, right_low, ahead, right_up, across_up, left_up)
    return out.transpose(0, 2, 1, 3)[None]


def solution(mesh):
    return jax.shard_map(
        local,
        mesh=mesh,
        in_specs=(
            P(("slab", "bal"), None, None, None),
            P(),
            P(),
            P(),
            P(("slab", "bal"), None, None),
            P(),
        ),
        out_specs=P(("slab", "bal"), None, None, None, None),
        check_vma=False,
    )
```

profile of v0, /device:TPU:96, one launch (start us, length us, event | category | flops | bytes accessed | tf_op | source)
XLA Modules:
  0.0 80.0 jit_solution(12500664651358349098)
XLA Ops:
  0.0 3.6 %collective-permute-start = (s32[3,1,6]{2,1,0:T(1,128)}, s32[3,1,6]{2,1,0:T(1,128)S(1)}, u32[]{:S(2)}, u32[]{:S(2)}) collective-permute-start(s32[3,1,6]{2,1,0:T(1,128)} %bitcast.8), channel_id=1, source_target_pairs={{0,1},{1,2},{2,3},{3,4},{4,5},{5,6},{6,7},{7,8},{8,9},{9,10},{10,1... | collective-permute-start | bytes 224 | tf_op jit(solution)/shard_map/ppermute | solution.py:644
  3.6 5.8 %collective-permute-done.prev_ref = s32[3,1,6]{2,1,0:T(1,128)S(1)} collective-permute-done((s32[3,1,6]{2,1,0:T(1,128)}, s32[3,1,6]{2,1,0:T(1,128)S(1)}, u32[]{:S(2)}, u32[]{:S(2)}) %collective-permute-start) | collective-permute-done | bytes 104 | tf_op jit(solution)/shard_map/ppermute | solution.py:644
  9.5 0.6 copy-done.1
  10.1 3.3 %gather.1 = (s32[9]{0:T(128)}, bf16[3,4,16,256]{3,2,1,0:T(8,128)(2,1)}, bf16[3,4,16,256]{3,2,1,0:T(8,128)(2,1)}, bf16[4,4,16,256]{3,2,1,0:T(8,128)(2,1)}, bf16[3...) custom-call(s32[1]{0:T(128)} %bitcast.column_ref, s32[3,1,6]{2,1,0:T(1,128)} %copy-done.1, s32[128]{0:T(128)} %count_hbm.1, ...), custom_call_target="tpu_custom_call" | custom-call | tf_op jit(solution)/shard_map/gather/pallas_call | solution.py:191
  13.4 1.9 %collective-permute-start.1 = (bf16[4,4,16,256]{3,2,1,0:T(8,128)(2,1)}, bf16[4,4,16,256]{3,2,1,0:T(8,128)(2,1)S(1)}, u32[]{:S(2)}, u32[]{:S(2)}) collective-permute-start(bf16[4,4,16,256]{3,2,1,0:T(8,128)(2,1)} %get-tuple-element.26), channel_id=1, source_target_pairs={{1,0},{2,1},{3,2},{4,3},{5,4},{6,5},{7,6},{8,7},{9,8},{10,9},{11,1... | collective-permute-start | bytes 393224 | tf_op jit(solution)/shard_map/ppermute | solution.py:644
  15.3 2.1 %collective-permute-start.2 = (bf16[3,4,16,256]{3,2,1,0:T(8,128)(2,1)}, bf16[3,4,16,256]{3,2,1,0:T(8,128)(2,1)S(1)}, u32[]{:S(2)}, u32[]{:S(2)}) collective-permute-start(bf16[3,4,16,256]{3,2,1,0:T(8,128)(2,1)} %get-tuple-element.27), channel_id=1, source_target_pairs={{0,1},{1,2},{2,3},{3,0},{4,5},{5,6},{6,7},{7,4},{8,9},{9,10},{10,1... | collective-permute-start | bytes 294920 | tf_op jit(solution)/shard_map/ppermute | solution.py:649
  17.4 1.9 %collective-permute-start.3 = (bf16[3,4,16,256]{3,2,1,0:T(8,128)(2,1)}, bf16[3,4,16,256]{3,2,1,0:T(8,128)(2,1)S(1)}, u32[]{:S(2)}, u32[]{:S(2)}) collective-permute-start(bf16[3,4,16,256]{3,2,1,0:T(8,128)(2,1)} %get-tuple-element.28.here_ref), channel_id=1, source_target_pairs={{4,0},{8,4},{12,8},{16,12},{20,16},{24,20},{28,24},{32,28},{36,32}... | collective-permute-start | bytes 294920 | tf_op jit(solution)/shard_map/ppermute | solution.py:656
  19.3 1.9 %collective-permute-start.4 = (bf16[1,4,16,256]{3,2,1,0:T(8,128)(2,1)}, bf16[1,4,16,256]{3,2,1,0:T(8,128)(2,1)S(1)}, u32[]{:S(2)}, u32[]{:S(2)}) collective-permute-start(bf16[1,4,16,256]{3,2,1,0:T(8,128)(2,1)} %get-tuple-element.29), channel_id=1, source_target_pairs={{2,0},{3,1},{4,2},{5,3},{6,4},{7,5},{8,6},{9,7},{10,8},{11,9},{12,... | collective-permute-start | bytes 98312 | tf_op jit(solution)/shard_map/ppermute | solution.py:644
  21.3 0.0 copy-start.5
  21.3 0.9 %copy-done.5 = bf16[3,3,3,32,32]{4,3,2,1,0:T(8,128)(2,1)S(1)} copy-done((bf16[3,3,3,32,32]{4,3,2,1,0:T(8,128)(2,1)S(1)}, bf16[3,3,3,32,32]{4,3,2,1,0:T(8,128)(2,1)}, u32[]{:S(2)}) %copy-start.5) | copy-done | bytes 55320
  22.2 0.7 copy-done.8
  22.9 0.7 copy-done.9
  23.6 0.8 %weights.1 = (bf16[6,256,256]{2,1,0:T(8,128)(2,1)S(1)}, bf16[2048,256]{1,0:T(8,128)(2,1)S(1)}, bf16[8,256,256]{2,1,0:T(8,128)(2,1)S(1)}) custom-call(bf16[3,3,3,32]{3,2,1,0:T(4,128)(2,1)S(1)} %copy-done.8, bf16[27,32,32]{2,1,0:T(8,128)(2,1)S(1)} %bitcast.11, bf16[3,32]{1,0:T(4,128)(2,1)S(1)} %bitcast.12), custom_call_target="tpu_custom_call" | custom-call | flops 1000000000 | bytes 8000000 | tf_op jit(solution)/shard_map/weights/pallas_call | solution.py:264
  24.4 2.4 %collective-permute-done.4.left_ref = bf16[1,4,16,256]{3,2,1,0:T(8,128)(2,1)S(1)} collective-permute-done((bf16[1,4,16,256]{3,2,1,0:T(8,128)(2,1)}, bf16[1,4,16,256]{3,2,1,0:T(8,128)(2,1)S(1)}, u32[]{:S(2)}, u32[]{:S(2)}) %collective-permute-start.4) | collective-permute-done | bytes 32800 | tf_op jit(solution)/shard_map/ppermute | solution.py:644
  26.9 0.0 collective-permute-done.2.right_ref
  26.9 0.0 collective-permute-done.3.across_ref
  26.9 0.0 collective-permute-done.1.back_ref
  26.9 0.0 copy-done.12
  26.9 0.6 copy-done.3
  27.5 0.9 %copy-done.6 = bf16[3,4,16,256]{3,2,1,0:T(8,128)(2,1)S(1)} copy-done((bf16[3,4,16,256]{3,2,1,0:T(8,128)(2,1)S(1)}, bf16[3,4,16,256]{3,2,1,0:T(8,128)(2,1)}, u32[]{:S(2)}) %copy-start.6) | copy-done | bytes 98328
  28.4 0.9 %copy-done.7 = bf16[3,4,16,256]{3,2,1,0:T(8,128)(2,1)S(1)} copy-done((bf16[3,4,16,256]{3,2,1,0:T(8,128)(2,1)S(1)}, bf16[3,4,16,256]{3,2,1,0:T(8,128)(2,1)}, u32[]{:S(2)}) %copy-start.7) | copy-done | bytes 98328
  29.3 28.3 %network.1 = (bf16[3,4,32,256]{3,2,1,0:T(8,128)(2,1)S(1)}, bf16[4,4,32,256]{3,2,1,0:T(8,128)(2,1)S(1)}, bf16[3,4,32,256]{3,2,1,0:T(8,128)(2,1)S(1)}, bf16[3,4,32...) custom-call(s32[9]{0:T(128)S(1)} %copy-done.3, bf16[3,4,16,256]{3,2,1,0:T(8,128)(2,1)S(1)} %copy-done.6, ...), custom_call_target="tpu_custom_call" | custom-call | flops 20000000000 | bytes 8000000 | tf_op jit(solution)/shard_map/network/pallas_call | solution.py:491
  57.6 1.9 %collective-permute-start.6 = (bf16[4,4,32,256]{3,2,1,0:T(8,128)(2,1)S(1)}, bf16[4,4,32,256]{3,2,1,0:T(8,128)(2,1)S(1)}, u32[]{:S(2)}, u32[]{:S(2)}) collective-permute-start(bf16[4,4,32,256]{3,2,1,0:T(8,128)(2,1)S(1)} %get-tuple-element.40), channel_id=1, source_target_pairs={{0,1},{1,2},{2,3},{3,4},{4,5},{5,6},{6,7},{7,8},{8,9},{9,10},{10,1... | collective-permute-start | bytes 786440 | tf_op jit(solution)/shard_map/ppermute | solution.py:644
  59.5 2.2 %collective-permute-start.5 = (bf16[3,4,32,256]{3,2,1,0:T(8,128)(2,1)S(1)}, bf16[3,4,32,256]{3,2,1,0:T(8,128)(2,1)S(1)}, u32[]{:S(2)}, u32[]{:S(2)}) collective-permute-start(bf16[3,4,32,256]{3,2,1,0:T(8,128)(2,1)S(1)} %get-tuple-element.39), channel_id=1, source_target_pairs={{0,3},{1,0},{2,1},{3,2},{4,7},{5,4},{6,5},{7,6},{8,11},{9,8},{10,9... | collective-permute-start | bytes 589832 | tf_op jit(solution)/shard_map/ppermute | solution.py:649
  61.8 1.9 %collective-permute-start.7 = (bf16[3,4,32,256]{3,2,1,0:T(8,128)(2,1)S(1)}, bf16[3,4,32,256]{3,2,1,0:T(8,128)(2,1)S(1)}, u32[]{:S(2)}, u32[]{:S(2)}) collective-permute-start(bf16[3,4,32,256]{3,2,1,0:T(8,128)(2,1)S(1)} %get-tuple-element.41.here_ref), channel_id=1, source_target_pairs={{0,4},{4,8},{8,12},{12,16},{16,20},{20,24},{24,28},{28,32},{32,36}... | collective-permute-start | bytes 589832 | tf_op jit(solution)/shard_map/ppermute | solution.py:656
  63.7 1.9 %collective-permute-start.8 = (bf16[1,4,32,256]{3,2,1,0:T(8,128)(2,1)S(1)}, bf16[1,4,32,256]{3,2,1,0:T(8,128)(2,1)S(1)}, u32[]{:S(2)}, u32[]{:S(2)}) collective-permute-start(bf16[1,4,32,256]{3,2,1,0:T(8,128)(2,1)S(1)} %get-tuple-element.42), channel_id=1, source_target_pairs={{0,2},{1,3},{2,4},{3,5},{4,6},{5,7},{6,8},{7,9},{8,10},{9,11},{10,... | collective-permute-start | bytes 196616 | tf_op jit(solution)/shard_map/ppermute | solution.py:644
  65.7 2.4 %inverse_weights.1 = (f32[256,4096]{1,0:T(8,128)S(1)}, bf16[256,128]{1,0:T(8,128)(2,1)S(1)}) custom-call(s32[9]{0:T(128)S(1)} %copy-done.4, s32[3,1,6]{2,1,0:T(1,128)S(1)} %bitcast.10, s32[3,1,6]{2,1,0:T(1,128)S(1)} %copy-done.2, bf16[256,4096]{1,0:T(8,128)(2,1)S(1)} %copy-done.10), custom_call_target="tpu_custom_call" | custom-call | flops 1000000000 | bytes 8000000 | tf_op jit(solution)/shard_map/inverse_weights/pallas_call | solution.py:542
  68.1 5.7 %collective-permute-done.8.left_ref = bf16[1,4,32,256]{3,2,1,0:T(8,128)(2,1)S(1)} collective-permute-done((bf16[1,4,32,256]{3,2,1,0:T(8,128)(2,1)S(1)}, bf16[1,4,32,256]{3,2,1,0:T(8,128)(2,1)S(1)}, u32[]{:S(2)}, u32[]{:S(2)}) %collective-permute-start.8) | collective-permute-done | bytes 65568 | tf_op jit(solution)/shard_map/ppermute | solution.py:644
  73.8 0.0 collective-permute-done.5.right_ref
  73.8 0.0 collective-permute-done.7.across_ref
  73.8 0.0 collective-permute-done.6.ahead_ref
  73.8 6.2 %blend.1 = f32[4,3,64,4096]{3,2,1,0:T(8,128)} custom-call(s32[9]{0:T(128)S(1)} %copy-done.4, bf16[256,128]{1,0:T(8,128)(2,1)S(1)} %get-tuple-element.36.chosen_ref, f32[256,4096]{1,0:T(8,128)S(1)} %get-tuple-element.37.inverse_ref, bf16[3,4,32,256]{3,2,1,0:T(8,128)(2,1)S(1)} %get-tuple-element.38.low_ref, ...), custom_call_target="tpu_custom_call" | custom-call | tf_op jit(solution)/shard_map/blend/pallas_call | solution.py:625
  (19 shorter events, 0.0 us)
Async XLA Ops:
  0.0 26.9 %copy-start.12 = (f32[256,128]{1,0:T(8,128)S(1)}, f32[256,128]{1,0:T(8,128)}, u32[]{:S(2)}) copy-start(f32[256,128]{1,0:T(8,128)} %constant.21.clone.refs_5_) | copy-start | bytes 393220
  0.0 26.9 %copy-start.11 = (bf16[256,384]{1,0:T(8,128)(2,1)S(1)}, bf16[256,384]{1,0:T(8,128)(2,1)}, u32[]{:S(2)}) copy-start(bf16[256,384]{1,0:T(8,128)(2,1)} %constant.20.clone.refs_1_) | copy-start | bytes 589828
  0.0 26.9 %copy-start.13 = (bf16[64,32]{1,0:T(8,128)(2,1)S(1)}, bf16[64,32]{1,0:T(8,128)(2,1)}, u32[]{:S(2)}) copy-start(bf16[64,32]{1,0:T(8,128)(2,1)} %constant.19.clone.refs_0_) | copy-start | bytes 12292
  0.0 9.5 %collective-permute-start = (s32[3,1,6]{2,1,0:T(1,128)}, s32[3,1,6]{2,1,0:T(1,128)S(1)}, u32[]{:S(2)}, u32[]{:S(2)}) collective-permute-start(s32[3,1,6]{2,1,0:T(1,128)} %bitcast.8), channel_id=1, source_target_pairs={{0,1},{1,2},{2,3},{3,4},{4,5},{5,6},{6,7},{7,8},{8,9},{9,10},{10,1... | collective-permute-start | bytes 224 | tf_op jit(solution)/shard_map/ppermute | solution.py:644
  9.5 0.6 copy-start.1
  13.4 13.5 %collective-permute-start.1 = (bf16[4,4,16,256]{3,2,1,0:T(8,128)(2,1)}, bf16[4,4,16,256]{3,2,1,0:T(8,128)(2,1)S(1)}, u32[]{:S(2)}, u32[]{:S(2)}) collective-permute-start(bf16[4,4,16,256]{3,2,1,0:T(8,128)(2,1)} %get-tuple-element.26), channel_id=1, source_target_pairs={{1,0},{2,1},{3,2},{4,3},{5,4},{6,5},{7,6},{8,7},{9,8},{10,9},{11,1... | collective-permute-start | bytes 393224 | tf_op jit(solution)/shard_map/ppermute | solution.py:644
  15.3 11.5 %collective-permute-start.2 = (bf16[3,4,16,256]{3,2,1,0:T(8,128)(2,1)}, bf16[3,4,16,256]{3,2,1,0:T(8,128)(2,1)S(1)}, u32[]{:S(2)}, u32[]{:S(2)}) collective-permute-start(bf16[3,4,16,256]{3,2,1,0:T(8,128)(2,1)} %get-tuple-element.27), channel_id=1, source_target_pairs={{0,1},{1,2},{2,3},{3,0},{4,5},{5,6},{6,7},{7,4},{8,9},{9,10},{10,1... | collective-permute-start | bytes 294920 | tf_op jit(solution)/shard_map/ppermute | solution.py:649
  17.4 9.4 %collective-permute-start.3 = (bf16[3,4,16,256]{3,2,1,0:T(8,128)(2,1)}, bf16[3,4,16,256]{3,2,1,0:T(8,128)(2,1)S(1)}, u32[]{:S(2)}, u32[]{:S(2)}) collective-permute-start(bf16[3,4,16,256]{3,2,1,0:T(8,128)(2,1)} %get-tuple-element.28.here_ref), channel_id=1, source_target_pairs={{4,0},{8,4},{12,8},{16,12},{20,16},{24,20},{28,24},{32,28},{36,32}... | collective-permute-start | bytes 294920 | tf_op jit(solution)/shard_map/ppermute | solution.py:656
  19.3 7.5 %collective-permute-start.4 = (bf16[1,4,16,256]{3,2,1,0:T(8,128)(2,1)}, bf16[1,4,16,256]{3,2,1,0:T(8,128)(2,1)S(1)}, u32[]{:S(2)}, u32[]{:S(2)}) collective-permute-start(bf16[1,4,16,256]{3,2,1,0:T(8,128)(2,1)} %get-tuple-element.29), channel_id=1, source_target_pairs={{2,0},{3,1},{4,2},{5,3},{6,4},{7,5},{8,6},{9,7},{10,8},{11,9},{12,... | collective-permute-start | bytes 98312 | tf_op jit(solution)/shard_map/ppermute | solution.py:644
  21.3 0.9 %copy-start.5 = (bf16[3,3,3,32,32]{4,3,2,1,0:T(8,128)(2,1)S(1)}, bf16[3,3,3,32,32]{4,3,2,1,0:T(8,128)(2,1)}, u32[]{:S(2)}) copy-start(bf16[3,3,3,32,32]{4,3,2,1,0:T(8,128)(2,1)} %param.12) | copy-start | bytes 165892
  22.2 0.7 copy-start.8
  22.9 0.7 copy-start.9
  26.9 0.6 copy-start.3
  27.5 0.9 %copy-start.6 = (bf16[3,4,16,256]{3,2,1,0:T(8,128)(2,1)S(1)}, bf16[3,4,16,256]{3,2,1,0:T(8,128)(2,1)}, u32[]{:S(2)}) copy-start(bf16[3,4,16,256]{3,2,1,0:T(8,128)(2,1)} %get-tuple-element.25.own_ref) | copy-start | bytes 294916
  28.4 0.9 %copy-start.7 = (bf16[3,4,16,256]{3,2,1,0:T(8,128)(2,1)S(1)}, bf16[3,4,16,256]{3,2,1,0:T(8,128)(2,1)}, u32[]{:S(2)}) copy-start(bf16[3,4,16,256]{3,2,1,0:T(8,128)(2,1)} %get-tuple-element.28.here_ref) | copy-start | bytes 294916
  29.3 36.4 %copy-start = (s32[1,6,3]{1,0,2:T(1,128)S(1)}, s32[1,6,3]{1,0,2:T(1,128)}, u32[]{:S(2)}) copy-start(s32[1,6,3]{1,0,2:T(1,128)} %param.14) | copy-start | bytes 220
  29.3 36.4 %copy-start.2 = (s32[3,1,6]{2,1,0:T(1,128)S(1)}, s32[3,1,6]{2,1,0:T(1,128)}, u32[]{:S(2)}) copy-start(s32[3,1,6]{2,1,0:T(1,128)} %copy-done.1) | copy-start | bytes 220
  29.3 36.4 %copy-start.4 = (s32[9]{0:T(128)S(1)}, s32[9]{0:T(128)}, u32[]{:S(2)}) copy-start(s32[9]{0:T(128)} %get-tuple-element.24.plan_ref) | copy-start | bytes 112
  29.3 36.4 %copy-start.10 = (bf16[256,4096]{1,0:T(8,128)(2,1)S(1)}, bf16[256,4096]{1,0:T(8,128)(2,1)}, u32[]{:S(2)}) copy-start(bf16[256,4096]{1,0:T(8,128)(2,1)} %constant.22.clone.parts_ref) | copy-start | bytes 6291460
  57.6 16.2 %collective-permute-start.6 = (bf16[4,4,32,256]{3,2,1,0:T(8,128)(2,1)S(1)}, bf16[4,4,32,256]{3,2,1,0:T(8,128)(2,1)S(1)}, u32[]{:S(2)}, u32[]{:S(2)}) collective-permute-start(bf16[4,4,32,256]{3,2,1,0:T(8,128)(2,1)S(1)} %get-tuple-element.40), channel_id=1, source_target_pairs={{0,1},{1,2},{2,3},{3,4},{4,5},{5,6},{6,7},{7,8},{8,9},{9,10},{10,1... | collective-permute-start | bytes 786440 | tf_op jit(solution)/shard_map/ppermute | solution.py:644
  59.5 14.3 %collective-permute-start.5 = (bf16[3,4,32,256]{3,2,1,0:T(8,128)(2,1)S(1)}, bf16[3,4,32,256]{3,2,1,0:T(8,128)(2,1)S(1)}, u32[]{:S(2)}, u32[]{:S(2)}) collective-permute-start(bf16[3,4,32,256]{3,2,1,0:T(8,128)(2,1)S(1)} %get-tuple-element.39), channel_id=1, source_target_pairs={{0,3},{1,0},{2,1},{3,2},{4,7},{5,4},{6,5},{7,6},{8,11},{9,8},{10,9... | collective-permute-start | bytes 589832 | tf_op jit(solution)/shard_map/ppermute | solution.py:649
  61.8 12.0 %collective-permute-start.7 = (bf16[3,4,32,256]{3,2,1,0:T(8,128)(2,1)S(1)}, bf16[3,4,32,256]{3,2,1,0:T(8,128)(2,1)S(1)}, u32[]{:S(2)}, u32[]{:S(2)}) collective-permute-start(bf16[3,4,32,256]{3,2,1,0:T(8,128)(2,1)S(1)} %get-tuple-element.41.here_ref), channel_id=1, source_target_pairs={{0,4},{4,8},{8,12},{12,16},{16,20},{20,24},{24,28},{28,32},{32,36}... | collective-permute-start | bytes 589832 | tf_op jit(solution)/shard_map/ppermute | solution.py:656
  63.7 10.1 %collective-permute-start.8 = (bf16[1,4,32,256]{3,2,1,0:T(8,128)(2,1)S(1)}, bf16[1,4,32,256]{3,2,1,0:T(8,128)(2,1)S(1)}, u32[]{:S(2)}, u32[]{:S(2)}) collective-permute-start(bf16[1,4,32,256]{3,2,1,0:T(8,128)(2,1)S(1)} %get-tuple-element.42), channel_id=1, source_target_pairs={{0,2},{1,3},{2,4},{3,5},{4,6},{5,7},{6,8},{7,9},{8,10},{9,11},{10,... | collective-permute-start | bytes 196616 | tf_op jit(solution)/shard_map/ppermute | solution.py:644
where the time goes:
time: 80.5 us; the launch traced here: 80 us
  Pallas kernels  41.1 us (51%)
  starting transfers between devices  19.4 us (24%)
  waiting for transfers between devices  14 us (17%)
  local copies, waits for them, and re-layouts  5.27 us (7%)
    pallas_call x1, Pallas kernels, network(): call(network_kernel, 32, out_shape=(halves(3), halves(4), halves(3), halv...  28.3 us
    ppermute x5, waiting for transfers between devices, passed_along(): return lax.ppermute(block, axis, route)  14 us
    ppermute x5, starting transfers between devices, passed_along(): return lax.ppermute(block, axis, route)  11.3 us
    pallas_call x1, Pallas kernels, blend(): call(blend_kernel, 28, out_shape=jax.ShapeDtypeStruct(shape, F32), in_spe...  6.16 us
    unnamed x28, local copies, waits for them, and re-layouts  5.27 us
    ppermute x2, starting transfers between devices, passed_round(): lax.ppermute(block, 'bal', [(i, (i + distance) % size) for i in range(siz...  4.33 us
    ppermute x2, starting transfers between devices, passed_over(): lax.ppermute(block, axes, pairs if forward else [(b, a) for a, b in pairs])  3.82 us
    pallas_call x1, Pallas kernels, gather(): call(gather_kernel, 58, out_shape=(jax.ShapeDtypeStruct((9,), jnp.int32),...  3.35 us
  transfers between devices with their start and end apart: 9, of which 3 were waited for; matrix products, arithmetic and copies ran while one was open for 0% of the time, Pallas kernels for 4%

commit v1 on v0

--- a/solution.py
+++ b/solution.py
@@ -190,7 +190,7 @@
 
     return call(
         gather_kernel,
-        58,
+        53,
         out_shape=(jax.ShapeDtypeStruct((9,), jnp.int32), tiles(3), tiles(3), tiles(4), tiles(3), tiles(1)),
         in_specs=[SMEM_SPEC] * 2 + [pl.BlockSpec(memory_space=pltpu.HBM)] * 3,
         out_specs=(SMEM_SPEC,) + (VMEM_SPEC,) * 5,
@@ -661,17 +661,19 @@
     column = lax.axis_index(axes).astype(jnp.int32)
     corners = patch_corners.transpose(2, 0, 1)
     prev_corners = passed_along(corners, axes, 1)
+    laid_out = prepare_weights(first_kernel, second_kernel, class_weights)
+    laid_out, prev_corners = lax.optimization_barrier((laid_out, prev_corners))
+    weights = (
+        jnp.asarray(select_x(), BF16),
+        jnp.asarray(select_window(), BF16),
+        *laid_out,
+        jnp.asarray(blend_rows(), F32),
+    )
     plan, own_kept, own_right, back, here, two_back = gather(column[None], patch_counts, corners, prev_corners, volume[0])
     right = passed_round(own_right, 1)
     back = passed_along(back, axes, -1)
     across = passed_over(here, False)
     left = passed_along(two_back, axes, -2)
-    weights = (
-        jnp.asarray(select_x(), BF16),
-        jnp.asarray(select_window(), BF16),
-        *prepare_weights(first_kernel, second_kernel, class_weights),
-        jnp.asarray(blend_rows(), F32),
-    )
     low, ahead, right_low, right_up, left_up = network(plan, (own_kept, back, right, here, across, left), weights)
     ahead = passed_along(ahead, axes, 1)
     right_low = passed_round(right_low, -1)

time: 80.5 us -> 78.3 us (0.973)
  local copies, waits for them, and re-layouts: 5.27 us -> 3.66 us
    ppermute x2, starting transfers between devices: 4.33 us -> 2.42 us  [passed_round(): lax.ppermute(block, 'bal', [(i, (i + distance) % size) for i in range(siz...]
    ppermute x5, starting transfers between devices: 11.3 us -> 13.2 us  [passed_along(): return lax.ppermute(block, axis, route)]
    unnamed x28 -> x18, local copies, waits for them, and re-layouts: 5.27 us -> 3.66 us
where the time goes in v1:
time: 78.3 us; the launch traced here: 77.7 us
  Pallas kernels  40.7 us (52%)
  starting transfers between devices  19.4 us (25%)
  waiting for transfers between devices  13.8 us (18%)
  local copies, waits for them, and re-layouts  3.66 us (5%)
    pallas_call x1, Pallas kernels, network(): call(network_kernel, 32, out_shape=(halves(3), halves(4), halves(3), halv...  28.3 us
    ppermute x5, waiting for transfers between devices, passed_along(): return lax.ppermute(block, axis, route)  13.8 us
    ppermute x5, starting transfers between devices, passed_along(): return lax.ppermute(block, axis, route)  13.2 us
    pallas_call x1, Pallas kernels, blend(): call(blend_kernel, 28, out_shape=jax.ShapeDtypeStruct(shape, F32), in_spe...  6.15 us
    ppermute x2, starting transfers between devices, passed_over(): lax.ppermute(block, axes, pairs if forward else [(b, a) for a, b in pairs])  3.82 us
    unnamed x18, local copies, waits for them, and re-layouts  3.66 us
    pallas_call x1, Pallas kernels, gather(): call(gather_kernel, 53, out_shape=(jax.ShapeDtypeStruct((9,), jnp.int32),...  2.96 us
    pallas_call x1, Pallas kernels, inverse_weights(): call(inverse_kernel, 12, grid=(4,), out_shape=(jax.ShapeDtypeStruct((TILE...  2.43 us
  transfers between devices with their start and end apart: 9, of which 3 were waited for; matrix products, arithmetic and copies ran while one was open for 0% of the time, Pallas kernels for 4%

profile of v1, /device:TPU:96, one launch (start us, length us, event | category | flops | bytes accessed | tf_op | source)
XLA Modules:
  0.0 77.7 jit_solution(13458235732812216000)
XLA Ops:
  0.0 3.6 %collective-permute-start = (s32[3,1,6]{2,1,0:T(1,128)}, s32[3,1,6]{2,1,0:T(1,128)S(1)}, u32[]{:S(2)}, u32[]{:S(2)}) collective-permute-start(s32[3,1,6]{2,1,0:T(1,128)} %bitcast.8), channel_id=1, source_target_pairs={{0,1},{1,2},{2,3},{3,4},{4,5},{5,6},{6,7},{7,8},{8,9},{9,10},{10,1... | collective-permute-start | bytes 224 | tf_op jit(solution)/shard_map/ppermute | solution.py:644
  3.6 0.0 copy-start.2
  3.6 0.9 %copy-done.2 = bf16[3,3,3,32,32]{4,3,2,1,0:T(8,128)(2,1)S(1)} copy-done((bf16[3,3,3,32,32]{4,3,2,1,0:T(8,128)(2,1)S(1)}, bf16[3,3,3,32,32]{4,3,2,1,0:T(8,128)(2,1)}, u32[]{:S(2)}) %copy-start.2) | copy-done | bytes 55320
  4.6 0.7 copy-done.3
  5.3 0.7 copy-done.4
  5.9 0.8 %weights.1 = (bf16[6,256,256]{2,1,0:T(8,128)(2,1)S(1)}, bf16[2048,256]{1,0:T(8,128)(2,1)S(1)}, bf16[8,256,256]{2,1,0:T(8,128)(2,1)S(1)}) custom-call(bf16[3,3,3,32]{3,2,1,0:T(4,128)(2,1)S(1)} %copy-done.3, bf16[27,32,32]{2,1,0:T(8,128)(2,1)S(1)} %bitcast.11, bf16[3,32]{1,0:T(4,128)(2,1)S(1)} %bitcast.12), custom_call_target="tpu_custom_call" | custom-call | flops 1000000000 | bytes 8000000 | tf_op jit(solution)/shard_map/weights/pallas_call | solution.py:264
  6.8 2.7 %collective-permute-done.prev_ref = s32[3,1,6]{2,1,0:T(1,128)S(1)} collective-permute-done((s32[3,1,6]{2,1,0:T(1,128)}, s32[3,1,6]{2,1,0:T(1,128)S(1)}, u32[]{:S(2)}, u32[]{:S(2)}) %collective-permute-start) | collective-permute-done | bytes 104 | tf_op jit(solution)/shard_map/ppermute | solution.py:644
  9.5 0.7 copy-done
  10.1 0.7 copy-done.1
  10.8 3.0 %gather.1 = (s32[9]{0:T(128)S(1)}, bf16[3,4,16,256]{3,2,1,0:T(8,128)(2,1)S(1)}, bf16[3,4,16,256]{3,2,1,0:T(8,128)(2,1)S(1)}, bf16[4,4,16,256]{3,2,1,0:T(8,128)(2...) custom-call(s32[1]{0:T(128)} %bitcast.column_ref, ...), custom_call_target="tpu_custom_call" | custom-call | tf_op jit(solution)/shard_map/gather/pallas_call | solution.py:191
  13.8 3.8 %collective-permute-start.1 = (bf16[4,4,16,256]{3,2,1,0:T(8,128)(2,1)S(1)}, bf16[4,4,16,256]{3,2,1,0:T(8,128)(2,1)S(1)}, u32[]{:S(2)}, u32[]{:S(2)}) collective-permute-start(bf16[4,4,16,256]{3,2,1,0:T(8,128)(2,1)S(1)} %get-tuple-element.34), channel_id=1, source_target_pairs={{1,0},{2,1},{3,2},{4,3},{5,4},{6,5},{7,6},{8,7},{9,8},{10,9},{11,1... | collective-permute-start | bytes 393224 | tf_op jit(solution)/shard_map/ppermute | solution.py:644
  17.6 0.2 collective-permute-start.2
  17.8 1.9 %collective-permute-start.3 = (bf16[3,4,16,256]{3,2,1,0:T(8,128)(2,1)S(1)}, bf16[3,4,16,256]{3,2,1,0:T(8,128)(2,1)S(1)}, u32[]{:S(2)}, u32[]{:S(2)}) collective-permute-start(bf16[3,4,16,256]{3,2,1,0:T(8,128)(2,1)S(1)} %get-tuple-element.36.here_ref), channel_id=1, source_target_pairs={{4,0},{8,4},{12,8},{16,12},{20,16},{24,20},{28,24},{32,28},{36,32}... | collective-permute-start | bytes 294920 | tf_op jit(solution)/shard_map/ppermute | solution.py:656
  19.7 1.9 %collective-permute-start.4 = (bf16[1,4,16,256]{3,2,1,0:T(8,128)(2,1)S(1)}, bf16[1,4,16,256]{3,2,1,0:T(8,128)(2,1)S(1)}, u32[]{:S(2)}, u32[]{:S(2)}) collective-permute-start(bf16[1,4,16,256]{3,2,1,0:T(8,128)(2,1)S(1)} %get-tuple-element.37), channel_id=1, source_target_pairs={{2,0},{3,1},{4,2},{5,3},{6,4},{7,5},{8,6},{9,7},{10,8},{11,9},{12,... | collective-permute-start | bytes 98312 | tf_op jit(solution)/shard_map/ppermute | solution.py:644
  21.6 5.4 %collective-permute-done.4.left_ref = bf16[1,4,16,256]{3,2,1,0:T(8,128)(2,1)S(1)} collective-permute-done((bf16[1,4,16,256]{3,2,1,0:T(8,128)(2,1)S(1)}, bf16[1,4,16,256]{3,2,1,0:T(8,128)(2,1)S(1)}, u32[]{:S(2)}, u32[]{:S(2)}) %collective-permute-start.4) | collective-permute-done | bytes 32800 | tf_op jit(solution)/shard_map/ppermute | solution.py:644
  27.0 0.0 collective-permute-done.2.right_ref
  27.0 0.0 collective-permute-done.3.across_ref
  27.0 0.0 collective-permute-done.1.back_ref
  27.0 0.0 copy-done.8
  27.0 0.0 copy-start.5
  27.0 28.3 %network.1 = (bf16[3,4,32,256]{3,2,1,0:T(8,128)(2,1)S(1)}, bf16[4,4,32,256]{3,2,1,0:T(8,128)(2,1)S(1)}, bf16[3,4,32,256]{3,2,1,0:T(8,128)(2,1)S(1)}, bf16[3,4,32...) custom-call(s32[9]{0:T(128)S(1)} %get-tuple-element.32.plan_ref, ...), custom_call_target="tpu_custom_call" | custom-call | flops 20000000000 | bytes 8000000 | tf_op jit(solution)/shard_map/network/pallas_call | solution.py:491
  55.4 1.9 %collective-permute-start.6 = (bf16[4,4,32,256]{3,2,1,0:T(8,128)(2,1)S(1)}, bf16[4,4,32,256]{3,2,1,0:T(8,128)(2,1)S(1)}, u32[]{:S(2)}, u32[]{:S(2)}) collective-permute-start(bf16[4,4,32,256]{3,2,1,0:T(8,128)(2,1)S(1)} %get-tuple-element.48), channel_id=1, source_target_pairs={{0,1},{1,2},{2,3},{3,4},{4,5},{5,6},{6,7},{7,8},{8,9},{9,10},{10,1... | collective-permute-start | bytes 786440 | tf_op jit(solution)/shard_map/ppermute | solution.py:644
  57.3 2.2 %collective-permute-start.5 = (bf16[3,4,32,256]{3,2,1,0:T(8,128)(2,1)S(1)}, bf16[3,4,32,256]{3,2,1,0:T(8,128)(2,1)S(1)}, u32[]{:S(2)}, u32[]{:S(2)}) collective-permute-start(bf16[3,4,32,256]{3,2,1,0:T(8,128)(2,1)S(1)} %get-tuple-element.47), channel_id=1, source_target_pairs={{0,3},{1,0},{2,1},{3,2},{4,7},{5,4},{6,5},{7,6},{8,11},{9,8},{10,9... | collective-permute-start | bytes 589832 | tf_op jit(solution)/shard_map/ppermute | solution.py:649
  59.5 1.9 %collective-permute-start.7 = (bf16[3,4,32,256]{3,2,1,0:T(8,128)(2,1)S(1)}, bf16[3,4,32,256]{3,2,1,0:T(8,128)(2,1)S(1)}, u32[]{:S(2)}, u32[]{:S(2)}) collective-permute-start(bf16[3,4,32,256]{3,2,1,0:T(8,128)(2,1)S(1)} %get-tuple-element.49.here_ref), channel_id=1, source_target_pairs={{0,4},{4,8},{8,12},{12,16},{16,20},{20,24},{24,28},{28,32},{32,36}... | collective-permute-start | bytes 589832 | tf_op jit(solution)/shard_map/ppermute | solution.py:656
  61.4 1.9 %collective-permute-start.8 = (bf16[1,4,32,256]{3,2,1,0:T(8,128)(2,1)S(1)}, bf16[1,4,32,256]{3,2,1,0:T(8,128)(2,1)S(1)}, u32[]{:S(2)}, u32[]{:S(2)}) collective-permute-start(bf16[1,4,32,256]{3,2,1,0:T(8,128)(2,1)S(1)} %get-tuple-element.50), channel_id=1, source_target_pairs={{0,2},{1,3},{2,4},{3,5},{4,6},{5,7},{6,8},{7,9},{8,10},{9,11},{10,... | collective-permute-start | bytes 196616 | tf_op jit(solution)/shard_map/ppermute | solution.py:644
  63.4 0.0 copy-done.5
  63.4 2.4 %inverse_weights.1 = (f32[256,4096]{1,0:T(8,128)S(1)}, bf16[256,128]{1,0:T(8,128)(2,1)S(1)}) custom-call(s32[9]{0:T(128)S(1)} %get-tuple-element.32.plan_ref, s32[3,1,6]{2,1,0:T(1,128)S(1)} %bitcast.10, s32[3,1,6]{2,1,0:T(1,128)S(1)} %collective-permute-done.prev_ref, bf16[256,4096]{1,0:T(8,128)(2,1)S(1)} %copy-done.5), custom_call_target="tpu_custom_call" | custom-call | flops 1000000000 | bytes 8000000 | tf_op jit(solution)/shard_map/inverse_weights/pallas_call | solution.py:542
  65.8 5.7 %collective-permute-done.8.left_ref = bf16[1,4,32,256]{3,2,1,0:T(8,128)(2,1)S(1)} collective-permute-done((bf16[1,4,32,256]{3,2,1,0:T(8,128)(2,1)S(1)}, bf16[1,4,32,256]{3,2,1,0:T(8,128)(2,1)S(1)}, u32[]{:S(2)}, u32[]{:S(2)}) %collective-permute-start.8) | collective-permute-done | bytes 65568 | tf_op jit(solution)/shard_map/ppermute | solution.py:644
  71.5 0.0 collective-permute-done.5.right_ref
  71.5 0.0 collective-permute-done.7.across_ref
  71.5 0.0 collective-permute-done.6.ahead_ref
  71.6 6.2 %blend.1 = f32[4,3,64,4096]{3,2,1,0:T(8,128)} custom-call(s32[9]{0:T(128)S(1)} %get-tuple-element.32.plan_ref, bf16[256,128]{1,0:T(8,128)(2,1)S(1)} %get-tuple-element.44.chosen_ref, f32[256,4096]{1,0:T(8,128)S(1)} %get-tuple-element.45.inverse_ref, bf16[3,4,32,256]{3,2,1,0:T(8,128)(2,1)S(1)} %get-tuple-element.46.low_ref, ...), custom_call_target="tpu_custom_call" | custom-call | tf_op jit(solution)/shard_map/blend/pallas_call | solution.py:625
  (9 shorter events, 0.0 us)
Async XLA Ops:
  0.0 27.0 %copy-start.8 = (bf16[64,32]{1,0:T(8,128)(2,1)S(1)}, bf16[64,32]{1,0:T(8,128)(2,1)}, u32[]{:S(2)}) copy-start(bf16[64,32]{1,0:T(8,128)(2,1)} %constant.19.clone.refs_0_) | copy-start | bytes 12292
  0.0 9.4 %collective-permute-start = (s32[3,1,6]{2,1,0:T(1,128)}, s32[3,1,6]{2,1,0:T(1,128)S(1)}, u32[]{:S(2)}, u32[]{:S(2)}) collective-permute-start(s32[3,1,6]{2,1,0:T(1,128)} %bitcast.8), channel_id=1, source_target_pairs={{0,1},{1,2},{2,3},{3,4},{4,5},{5,6},{6,7},{7,8},{8,9},{9,10},{10,1... | collective-permute-start | bytes 224 | tf_op jit(solution)/shard_map/ppermute | solution.py:644
  3.6 0.9 %copy-start.2 = (bf16[3,3,3,32,32]{4,3,2,1,0:T(8,128)(2,1)S(1)}, bf16[3,3,3,32,32]{4,3,2,1,0:T(8,128)(2,1)}, u32[]{:S(2)}) copy-start(bf16[3,3,3,32,32]{4,3,2,1,0:T(8,128)(2,1)} %param.12) | copy-start | bytes 165892
  4.6 0.7 copy-start.3
  5.3 0.7 copy-start.4
  5.9 21.1 %copy-start.6 = (bf16[256,384]{1,0:T(8,128)(2,1)S(1)}, bf16[256,384]{1,0:T(8,128)(2,1)}, u32[]{:S(2)}) copy-start(bf16[256,384]{1,0:T(8,128)(2,1)} %constant.20.clone.refs_1_) | copy-start | bytes 589828
  5.9 21.1 %copy-start.7 = (f32[256,128]{1,0:T(8,128)S(1)}, f32[256,128]{1,0:T(8,128)}, u32[]{:S(2)}) copy-start(f32[256,128]{1,0:T(8,128)} %constant.21.clone.refs_5_) | copy-start | bytes 393220
  9.5 0.7 copy-start
  10.1 0.7 copy-start.1
  13.8 13.2 %collective-permute-start.1 = (bf16[4,4,16,256]{3,2,1,0:T(8,128)(2,1)S(1)}, bf16[4,4,16,256]{3,2,1,0:T(8,128)(2,1)S(1)}, u32[]{:S(2)}, u32[]{:S(2)}) collective-permute-start(bf16[4,4,16,256]{3,2,1,0:T(8,128)(2,1)S(1)} %get-tuple-element.34), channel_id=1, source_target_pairs={{1,0},{2,1},{3,2},{4,3},{5,4},{6,5},{7,6},{8,7},{9,8},{10,9},{11,1... | collective-permute-start | bytes 393224 | tf_op jit(solution)/shard_map/ppermute | solution.py:644
  17.6 9.4 %collective-permute-start.2 = (bf16[3,4,16,256]{3,2,1,0:T(8,128)(2,1)S(1)}, bf16[3,4,16,256]{3,2,1,0:T(8,128)(2,1)S(1)}, u32[]{:S(2)}, u32[]{:S(2)}) collective-permute-start(bf16[3,4,16,256]{3,2,1,0:T(8,128)(2,1)S(1)} %get-tuple-element.35), channel_id=1, source_target_pairs={{0,1},{1,2},{2,3},{3,0},{4,5},{5,6},{6,7},{7,4},{8,9},{9,10},{10,1... | collective-permute-start | bytes 294920 | tf_op jit(solution)/shard_map/ppermute | solution.py:649
  17.8 9.2 %collective-permute-start.3 = (bf16[3,4,16,256]{3,2,1,0:T(8,128)(2,1)S(1)}, bf16[3,4,16,256]{3,2,1,0:T(8,128)(2,1)S(1)}, u32[]{:S(2)}, u32[]{:S(2)}) collective-permute-start(bf16[3,4,16,256]{3,2,1,0:T(8,128)(2,1)S(1)} %get-tuple-element.36.here_ref), channel_id=1, source_target_pairs={{4,0},{8,4},{12,8},{16,12},{20,16},{24,20},{28,24},{32,28},{36,32}... | collective-permute-start | bytes 294920 | tf_op jit(solution)/shard_map/ppermute | solution.py:656
  19.7 7.3 %collective-permute-start.4 = (bf16[1,4,16,256]{3,2,1,0:T(8,128)(2,1)S(1)}, bf16[1,4,16,256]{3,2,1,0:T(8,128)(2,1)S(1)}, u32[]{:S(2)}, u32[]{:S(2)}) collective-permute-start(bf16[1,4,16,256]{3,2,1,0:T(8,128)(2,1)S(1)} %get-tuple-element.37), channel_id=1, source_target_pairs={{2,0},{3,1},{4,2},{5,3},{6,4},{7,5},{8,6},{9,7},{10,8},{11,9},{12,... | collective-permute-start | bytes 98312 | tf_op jit(solution)/shard_map/ppermute | solution.py:644
  27.0 36.3 %copy-start.5 = (bf16[256,4096]{1,0:T(8,128)(2,1)S(1)}, bf16[256,4096]{1,0:T(8,128)(2,1)}, u32[]{:S(2)}) copy-start(bf16[256,4096]{1,0:T(8,128)(2,1)} %constant.22.clone.parts_ref) | copy-start | bytes 6291460
  55.4 16.2 %collective-permute-start.6 = (bf16[4,4,32,256]{3,2,1,0:T(8,128)(2,1)S(1)}, bf16[4,4,32,256]{3,2,1,0:T(8,128)(2,1)S(1)}, u32[]{:S(2)}, u32[]{:S(2)}) collective-permute-start(bf16[4,4,32,256]{3,2,1,0:T(8,128)(2,1)S(1)} %get-tuple-element.48), channel_id=1, source_target_pairs={{0,1},{1,2},{2,3},{3,4},{4,5},{5,6},{6,7},{7,8},{8,9},{9,10},{10,1... | collective-permute-start | bytes 786440 | tf_op jit(solution)/shard_map/ppermute | solution.py:644
  57.3 14.3 %collective-permute-start.5 = (bf16[3,4,32,256]{3,2,1,0:T(8,128)(2,1)S(1)}, bf16[3,4,32,256]{3,2,1,0:T(8,128)(2,1)S(1)}, u32[]{:S(2)}, u32[]{:S(2)}) collective-permute-start(bf16[3,4,32,256]{3,2,1,0:T(8,128)(2,1)S(1)} %get-tuple-element.47), channel_id=1, source_target_pairs={{0,3},{1,0},{2,1},{3,2},{4,7},{5,4},{6,5},{7,6},{8,11},{9,8},{10,9... | collective-permute-start | bytes 589832 | tf_op jit(solution)/shard_map/ppermute | solution.py:649
  59.5 12.0 %collective-permute-start.7 = (bf16[3,4,32,256]{3,2,1,0:T(8,128)(2,1)S(1)}, bf16[3,4,32,256]{3,2,1,0:T(8,128)(2,1)S(1)}, u32[]{:S(2)}, u32[]{:S(2)}) collective-permute-start(bf16[3,4,32,256]{3,2,1,0:T(8,128)(2,1)S(1)} %get-tuple-element.49.here_ref), channel_id=1, source_target_pairs={{0,4},{4,8},{8,12},{12,16},{16,20},{20,24},{24,28},{28,32},{32,36}... | collective-permute-start | bytes 589832 | tf_op jit(solution)/shard_map/ppermute | solution.py:656
  61.4 10.1 %collective-permute-start.8 = (bf16[1,4,32,256]{3,2,1,0:T(8,128)(2,1)S(1)}, bf16[1,4,32,256]{3,2,1,0:T(8,128)(2,1)S(1)}, u32[]{:S(2)}, u32[]{:S(2)}) collective-permute-start(bf16[1,4,32,256]{3,2,1,0:T(8,128)(2,1)S(1)} %get-tuple-element.50), channel_id=1, source_target_pairs={{0,2},{1,3},{2,4},{3,5},{4,6},{5,7},{6,8},{7,9},{8,10},{9,11},{10,... | collective-permute-start | bytes 196616 | tf_op jit(solution)/shard_map/ppermute | solution.py:644

commit v2 on v1

--- a/solution.py
+++ b/solution.py
@@ -166,52 +166,51 @@
 
 
 def gather_kernel(
-    column_ref, prev_ref, count_hbm, own_hbm, volume_hbm,
-    plan_ref, kept_out, right_out, back_out, here_out, two_back_out,
-    flat, own_left, sent, count_ref, own_ref, volume_ref, arrived,
+    plan_ref, own_ref, prev_ref, volume_hbm,
+    kept_out, right_out, back_out, here_out, two_back_out,
+    flat, own_left, volume_ref, arrived,
 ):
-    count_copy = pltpu.make_async_copy(count_hbm, count_ref, arrived.at[4])
-    own_copy = pltpu.make_async_copy(own_hbm, own_ref, arrived.at[5])
     copies = [pltpu.make_async_copy(volume_hbm.at[ty], volume_ref.at[ty], arrived.at[ty]) for ty in range(TILES_Y)]
-    for copy in [count_copy, own_copy] + copies:
+    for copy in copies:
         copy.start()
-    count_copy.wait()
-    write_plan(column_ref, count_ref, plan_ref, sent)
-    own_copy.wait()
     flatten(volume_ref, copies, flat)
     take_entries(plan_ref, 0, own_ref, flat, kept_out, right_out, own_left)
     take_entries(plan_ref, 3, prev_ref, flat, back_out, here_out, two_back_out)
     back_out[3] = own_left[0]
 
 
-def gather(column, patch_counts, corners, prev_corners, volume):
+def gather(plan, corners, prev_corners, volume):
     def tiles(count):
         return jax.ShapeDtypeStruct((count, 4, 16, 256), BF16)
 
     return call(
         gather_kernel,
         53,
-        out_shape=(jax.ShapeDtypeStruct((9,), jnp.int32), tiles(3), tiles(3), tiles(4), tiles(3), tiles(1)),
-        in_specs=[SMEM_SPEC] * 2 + [pl.BlockSpec(memory_space=pltpu.HBM)] * 3,
-        out_specs=(SMEM_SPEC,) + (VMEM_SPEC,) * 5,
+        out_shape=(tiles(3), tiles(3), tiles(4), tiles(3), tiles(1)),
+        in_specs=[SMEM_SPEC] * 3 + [pl.BlockSpec(memory_space=pltpu.HBM)],
+        out_specs=(VMEM_SPEC,) * 5,
         scratch_shapes=[
             pltpu.VMEM((TILES_Y * TILES_Z * 32, 128), F32),
             pltpu.VMEM((1, 4, 16, 256), BF16),
-            pltpu.SMEM((16,), jnp.int32),
-            pltpu.SMEM(patch_counts.shape, jnp.int32),
-            pltpu.SMEM(corners.shape, jnp.int32),
             pltpu.VMEM((TILES_Y, TILES_Z, TILE_VOX), BF16),
-            pltpu.SemaphoreType.DMA((6,)),
+            pltpu.SemaphoreType.DMA((TILES_Y,)),
         ],
         name="gather",
-    )(column, prev_corners, patch_counts, corners, volume)
+    )(plan, corners, prev_corners, volume)
 
 
 def dot(a, b):
     return jnp.dot(a, b, preferred_element_type=F32)
 
 
-def weights_kernel(first_ref, second_ref, class_ref, first_out, second_out, class_out, four, taps, turned):
+def weights_kernel(
+    column_ref, count_ref, corner_ref, first_ref, second_ref, class_ref,
+    plan_ref, corner_out, first_out, second_out, class_out, four, taps, turned, sent,
+):
+    write_plan(column_ref, count_ref, plan_ref, sent)
+    for i in range(3):
+        for slot in range(HOME_MOST):
+            corner_out[i, 0, slot] = corner_ref[i, 0, slot]
     lane = lax.broadcasted_iota(jnp.int32, (32, 256), 1)
     taps[...] = jnp.zeros((32, 32), F32)
     for dx in range(3):
@@ -260,21 +259,28 @@
             class_out[b, 32 * s : 32 * s + 32, :] = jnp.where(lane % 64 == place, columns, 0.0).astype(BF16)
 
 
-def prepare_weights(first_kernel, second_kernel, class_weights):
+def prepare(column, patch_counts, corners, first_kernel, second_kernel, class_weights):
     return call(
         weights_kernel,
         12,
         out_shape=(
+            jax.ShapeDtypeStruct((9,), jnp.int32),
+            jax.ShapeDtypeStruct(corners.shape, jnp.int32),
             jax.ShapeDtypeStruct((6, 256, 256), BF16),
             jax.ShapeDtypeStruct((2048, 256), BF16),
             jax.ShapeDtypeStruct((8, 256, 256), BF16),
         ),
-        in_specs=[VMEM_SPEC] * 3,
-        out_specs=(VMEM_SPEC,) * 3,
-        scratch_shapes=[pltpu.VMEM((27, 32, 128), F32), pltpu.VMEM((32, 32), F32), pltpu.VMEM((128, 128), F32)],
+        in_specs=[SMEM_SPEC] * 3 + [VMEM_SPEC] * 3,
+        out_specs=(SMEM_SPEC,) * 2 + (VMEM_SPEC,) * 3,
+        scratch_shapes=[
+            pltpu.VMEM((27, 32, 128), F32),
+            pltpu.VMEM((32, 32), F32),
+            pltpu.VMEM((128, 128), F32),
+            pltpu.SMEM((16,), jnp.int32),
+        ],
         cost_estimate=pl.CostEstimate(flops=1_000_000_000, bytes_accessed=8_000_000, transcendentals=0),
         name="weights",
-    )(first_kernel, second_kernel.reshape(27, CHANNELS, CHANNELS), class_weights.T)
+    )(column, patch_counts, corners, first_kernel, second_kernel.reshape(27, CHANNELS, CHANNELS), class_weights.T)
 
 
 def fold_channels(row):
@@ -661,15 +667,15 @@
     column = lax.axis_index(axes).astype(jnp.int32)
     corners = patch_corners.transpose(2, 0, 1)
     prev_corners = passed_along(corners, axes, 1)
-    laid_out = prepare_weights(first_kernel, second_kernel, class_weights)
-    laid_out, prev_corners = lax.optimization_barrier((laid_out, prev_corners))
+    prepared = prepare(column[None], patch_counts, corners, first_kernel, second_kernel, class_weights)
+    (plan, corners, *laid_out), prev_corners = lax.optimization_barrier((prepared, prev_corners))
     weights = (
         jnp.asarray(select_x(), BF16),
         jnp.asarray(select_window(), BF16),
         *laid_out,
         jnp.asarray(blend_rows(), F32),
     )
-    plan, own_kept, own_right, back, here, two_back = gather(column[None], patch_counts, corners, prev_corners, volume[0])
+    own_kept, own_right, back, here, two_back = gather(plan, corners, prev_corners, volume[0])
     right = passed_round(own_right, 1)
     back = passed_along(back, axes, -1)
     across = passed_over(here, False)

time: 78.3 us -> 78.7 us (level)
  waiting for transfers between devices: 13.8 us -> 11.3 us
  starting transfers between devices: 19.4 us -> 21.6 us
  Pallas kernels: 40.7 us -> 41.6 us
    ppermute x5, waiting for transfers between devices: 13.8 us -> 11.3 us  [passed_along(): return lax.ppermute(block, axis, route)]
    ppermute x5, starting transfers between devices: 13.2 us -> 15.4 us  [passed_along(): return lax.ppermute(block, axis, route)]
    pallas_call x2, Pallas kernels: 3.79 us -> 4.64 us  [the longest x1 2.64 us: gather(): call(gather_kernel, 53, out_shape=(tiles(3), tiles(3), tiles(4), tiles(3)...]
  transfers between devices with their start and end apart: 9 -> 9, of which waited for: 3 -> 3; matrix products, arithmetic and copies ran while one was open for 0% -> 0% of each run, Pallas kernels for 4% -> 6%
where the time goes in v2:
time: 78.7 us; the launch traced here: 78.3 us
  Pallas kernels  41.6 us (53%)
  starting transfers between devices  21.6 us (27%)
  waiting for transfers between devices  11.3 us (14%)
  local copies, waits for them, and re-layouts  3.66 us (5%)
    pallas_call x1, Pallas kernels, network(): call(network_kernel, 32, out_shape=(halves(3), halves(4), halves(3), halv...  28.4 us
    ppermute x5, starting transfers between devices, passed_along(): return lax.ppermute(block, axis, route)  15.4 us
    ppermute x5, waiting for transfers between devices, passed_along(): return lax.ppermute(block, axis, route)  11.3 us
    pallas_call x1, Pallas kernels, blend(): call(blend_kernel, 28, out_shape=jax.ShapeDtypeStruct(shape, F32), in_spe...  6.16 us
    ppermute x2, starting transfers between devices, passed_over(): lax.ppermute(block, axes, pairs if forward else [(b, a) for a, b in pairs])  3.83 us
    unnamed x18, local copies, waits for them, and re-layouts  3.66 us
    pallas_call x1, Pallas kernels, gather(): call(gather_kernel, 53, out_shape=(tiles(3), tiles(3), tiles(4), tiles(3)...  2.64 us
    pallas_call x1, Pallas kernels, inverse_weights(): call(inverse_kernel, 12, grid=(4,), out_shape=(jax.ShapeDtypeStruct((TILE...  2.43 us
  transfers between devices with their start and end apart: 9, of which 3 were waited for; matrix products, arithmetic and copies ran while one was open for 0% of the time, Pallas kernels for 6%

profile of v2, /device:TPU:96, one launch (start us, length us, event | category | flops | bytes accessed | tf_op | source)
XLA Modules:
  0.0 78.3 jit_solution(11043588286268637507)
XLA Ops:
  0.0 3.6 %collective-permute-start = (s32[3,1,6]{2,1,0:T(1,128)}, s32[3,1,6]{2,1,0:T(1,128)S(1)}, u32[]{:S(2)}, u32[]{:S(2)}) collective-permute-start(s32[3,1,6]{2,1,0:T(1,128)} %bitcast.9), channel_id=1, source_target_pairs={{0,1},{1,2},{2,3},{3,4},{4,5},{5,6},{6,7},{7,8},{8,9},{9,10},{10,1... | collective-permute-start | bytes 224 | tf_op jit(solution)/shard_map/ppermute | solution.py:650
  3.6 0.0 copy-start
  3.6 0.9 %copy-done = bf16[3,3,3,32,32]{4,3,2,1,0:T(8,128)(2,1)S(1)} copy-done((bf16[3,3,3,32,32]{4,3,2,1,0:T(8,128)(2,1)S(1)}, bf16[3,3,3,32,32]{4,3,2,1,0:T(8,128)(2,1)}, u32[]{:S(2)}) %copy-start) | copy-done | bytes 55320
  4.6 0.7 copy-done.1
  5.3 0.7 copy-done.2
  5.9 0.7 copy-done.3
  6.6 0.7 copy-done.4
  7.3 2.0 %weights.1 = (s32[9]{0:T(128)S(1)}, s32[3,1,6]{2,1,0:T(1,128)S(1)}, bf16[6,256,256]{2,1,0:T(8,128)(2,1)S(1)}, bf16[2048,256]{1,0:T(8,128)(2,1)S(1)}, bf16[8,256,256]{2,1,0:T(8,128)(2,1)S(1)}) custom-call(s32[1]{0:T(128)} %bitcast.column_ref, s32[128]{0:T(128)S(1)} %copy-done.4, s32[3,1,6]{2,1,0:T(1,128)S(1)} %bitcast.10, ...), custom_call_target="tpu_custom_call" | custom-call | flops 1000000000 | bytes 8000000 | tf_op jit(solution)/shard_map/weights/pallas_call | solution.py:263
  9.3 0.2 collective-permute-done.prev_ref
  9.4 2.6 %gather.1 = (bf16[3,4,16,256]{3,2,1,0:T(8,128)(2,1)S(1)}, bf16[3,4,16,256]{3,2,1,0:T(8,128)(2,1)S(1)}, bf16[4,4,16,256]{3,2,1,0:T(8,128)(2,1)S(1)}, bf16[3,4,16,...) custom-call(s32[9]{0:T(128)S(1)} %get-tuple-element.36.plan_ref, s32[3,1,6]{2,1,0:T(1,128)S(1)} %get-tuple-element.48.own_ref, ...), custom_call_target="tpu_custom_call" | custom-call | tf_op jit(solution)/shard_map/gather/pallas_call | solution.py:186
  12.1 6.1 %collective-permute-start.1 = (bf16[4,4,16,256]{3,2,1,0:T(8,128)(2,1)S(1)}, bf16[4,4,16,256]{3,2,1,0:T(8,128)(2,1)S(1)}, u32[]{:S(2)}, u32[]{:S(2)}) collective-permute-start(bf16[4,4,16,256]{3,2,1,0:T(8,128)(2,1)S(1)} %get-tuple-element.40), channel_id=1, source_target_pairs={{1,0},{2,1},{3,2},{4,3},{5,4},{6,5},{7,6},{8,7},{9,8},{10,9},{11,1... | collective-permute-start | bytes 393224 | tf_op jit(solution)/shard_map/ppermute | solution.py:650
  18.2 0.1 collective-permute-start.2
  18.2 1.9 %collective-permute-start.3 = (bf16[3,4,16,256]{3,2,1,0:T(8,128)(2,1)S(1)}, bf16[3,4,16,256]{3,2,1,0:T(8,128)(2,1)S(1)}, u32[]{:S(2)}, u32[]{:S(2)}) collective-permute-start(bf16[3,4,16,256]{3,2,1,0:T(8,128)(2,1)S(1)} %get-tuple-element.42.here_ref), channel_id=1, source_target_pairs={{4,0},{8,4},{12,8},{16,12},{20,16},{24,20},{28,24},{32,28},{36,32}... | collective-permute-start | bytes 294920 | tf_op jit(solution)/shard_map/ppermute | solution.py:662
  20.2 1.9 %collective-permute-start.4 = (bf16[1,4,16,256]{3,2,1,0:T(8,128)(2,1)S(1)}, bf16[1,4,16,256]{3,2,1,0:T(8,128)(2,1)S(1)}, u32[]{:S(2)}, u32[]{:S(2)}) collective-permute-start(bf16[1,4,16,256]{3,2,1,0:T(8,128)(2,1)S(1)} %get-tuple-element.43), channel_id=1, source_target_pairs={{2,0},{3,1},{4,2},{5,3},{6,4},{7,5},{8,6},{9,7},{10,8},{11,9},{12,... | collective-permute-start | bytes 98312 | tf_op jit(solution)/shard_map/ppermute | solution.py:650
  22.1 5.4 %collective-permute-done.4.left_ref = bf16[1,4,16,256]{3,2,1,0:T(8,128)(2,1)S(1)} collective-permute-done((bf16[1,4,16,256]{3,2,1,0:T(8,128)(2,1)S(1)}, bf16[1,4,16,256]{3,2,1,0:T(8,128)(2,1)S(1)}, u32[]{:S(2)}, u32[]{:S(2)}) %collective-permute-start.4) | collective-permute-done | bytes 32800 | tf_op jit(solution)/shard_map/ppermute | solution.py:650
  27.5 0.0 collective-permute-done.2.right_ref
  27.5 0.0 collective-permute-done.3.across_ref
  27.5 0.0 collective-permute-done.1.back_ref
  27.5 0.0 copy-done.8
  27.5 0.0 copy-start.5
  27.5 28.4 %network.1 = (bf16[3,4,32,256]{3,2,1,0:T(8,128)(2,1)S(1)}, bf16[4,4,32,256]{3,2,1,0:T(8,128)(2,1)S(1)}, bf16[3,4,32,256]{3,2,1,0:T(8,128)(2,1)S(1)}, bf16[3,4,32...) custom-call(s32[9]{0:T(128)S(1)} %get-tuple-element.36.plan_ref, ...), custom_call_target="tpu_custom_call" | custom-call | flops 20000000000 | bytes 8000000 | tf_op jit(solution)/shard_map/network/pallas_call | solution.py:497
  55.9 1.9 %collective-permute-start.6 = (bf16[4,4,32,256]{3,2,1,0:T(8,128)(2,1)S(1)}, bf16[4,4,32,256]{3,2,1,0:T(8,128)(2,1)S(1)}, u32[]{:S(2)}, u32[]{:S(2)}) collective-permute-start(bf16[4,4,32,256]{3,2,1,0:T(8,128)(2,1)S(1)} %get-tuple-element.54), channel_id=1, source_target_pairs={{0,1},{1,2},{2,3},{3,4},{4,5},{5,6},{6,7},{7,8},{8,9},{9,10},{10,1... | collective-permute-start | bytes 786440 | tf_op jit(solution)/shard_map/ppermute | solution.py:650
  57.8 2.2 %collective-permute-start.5 = (bf16[3,4,32,256]{3,2,1,0:T(8,128)(2,1)S(1)}, bf16[3,4,32,256]{3,2,1,0:T(8,128)(2,1)S(1)}, u32[]{:S(2)}, u32[]{:S(2)}) collective-permute-start(bf16[3,4,32,256]{3,2,1,0:T(8,128)(2,1)S(1)} %get-tuple-element.53), channel_id=1, source_target_pairs={{0,3},{1,0},{2,1},{3,2},{4,7},{5,4},{6,5},{7,6},{8,11},{9,8},{10,9... | collective-permute-start | bytes 589832 | tf_op jit(solution)/shard_map/ppermute | solution.py:655
  60.1 1.9 %collective-permute-start.7 = (bf16[3,4,32,256]{3,2,1,0:T(8,128)(2,1)S(1)}, bf16[3,4,32,256]{3,2,1,0:T(8,128)(2,1)S(1)}, u32[]{:S(2)}, u32[]{:S(2)}) collective-permute-start(bf16[3,4,32,256]{3,2,1,0:T(8,128)(2,1)S(1)} %get-tuple-element.55.here_ref), channel_id=1, source_target_pairs={{0,4},{4,8},{8,12},{12,16},{16,20},{20,24},{24,28},{28,32},{32,36}... | collective-permute-start | bytes 589832 | tf_op jit(solution)/shard_map/ppermute | solution.py:662
  62.0 1.9 %collective-permute-start.8 = (bf16[1,4,32,256]{3,2,1,0:T(8,128)(2,1)S(1)}, bf16[1,4,32,256]{3,2,1,0:T(8,128)(2,1)S(1)}, u32[]{:S(2)}, u32[]{:S(2)}) collective-permute-start(bf16[1,4,32,256]{3,2,1,0:T(8,128)(2,1)S(1)} %get-tuple-element.56), channel_id=1, source_target_pairs={{0,2},{1,3},{2,4},{3,5},{4,6},{5,7},{6,8},{7,9},{8,10},{9,11},{10,... | collective-permute-start | bytes 196616 | tf_op jit(solution)/shard_map/ppermute | solution.py:650
  63.9 0.0 copy-done.5
  63.9 2.4 %inverse_weights.1 = (f32[256,4096]{1,0:T(8,128)S(1)}, bf16[256,128]{1,0:T(8,128)(2,1)S(1)}) custom-call(s32[9]{0:T(128)S(1)} %get-tuple-element.36.plan_ref, s32[3,1,6]{2,1,0:T(1,128)S(1)} %get-tuple-element.48.own_ref, s32[3,1,6]{2,1,0:T(1,128)S(1)} %collective-permute-done.prev_ref, bf16[256,4096]{1,0:T(8,128)(2,1)S(1)} %copy-done.5), custom_call_target="tpu_custom_call" | custom-call | flops 1000000000 | bytes 8000000 | tf_op jit(solution)/shard_map/inverse_weights/pallas_call | solution.py:548
  66.4 5.7 %collective-permute-done.8.left_ref = bf16[1,4,32,256]{3,2,1,0:T(8,128)(2,1)S(1)} collective-permute-done((bf16[1,4,32,256]{3,2,1,0:T(8,128)(2,1)S(1)}, bf16[1,4,32,256]{3,2,1,0:T(8,128)(2,1)S(1)}, u32[]{:S(2)}, u32[]{:S(2)}) %collective-permute-start.8) | collective-permute-done | bytes 65568 | tf_op jit(solution)/shard_map/ppermute | solution.py:650
  72.1 0.0 collective-permute-done.5.right_ref
  72.1 0.0 collective-permute-done.7.across_ref
  72.1 0.0 collective-permute-done.6.ahead_ref
  72.1 6.2 %blend.1 = f32[4,3,64,4096]{3,2,1,0:T(8,128)} custom-call(s32[9]{0:T(128)S(1)} %get-tuple-element.36.plan_ref, bf16[256,128]{1,0:T(8,128)(2,1)S(1)} %get-tuple-element.50.chosen_ref, f32[256,4096]{1,0:T(8,128)S(1)} %get-tuple-element.51.inverse_ref, bf16[3,4,32,256]{3,2,1,0:T(8,128)(2,1)S(1)} %get-tuple-element.52.low_ref, ...), custom_call_target="tpu_custom_call" | custom-call | tf_op jit(solution)/shard_map/blend/pallas_call | solution.py:631
  (9 shorter events, 0.0 us)
Async XLA Ops:
  0.0 27.5 %copy-start.8 = (bf16[64,32]{1,0:T(8,128)(2,1)S(1)}, bf16[64,32]{1,0:T(8,128)(2,1)}, u32[]{:S(2)}) copy-start(bf16[64,32]{1,0:T(8,128)(2,1)} %constant.19.clone.refs_0_) | copy-start | bytes 12292
  0.0 9.4 %collective-permute-start = (s32[3,1,6]{2,1,0:T(1,128)}, s32[3,1,6]{2,1,0:T(1,128)S(1)}, u32[]{:S(2)}, u32[]{:S(2)}) collective-permute-start(s32[3,1,6]{2,1,0:T(1,128)} %bitcast.9), channel_id=1, source_target_pairs={{0,1},{1,2},{2,3},{3,4},{4,5},{5,6},{6,7},{7,8},{8,9},{9,10},{10,1... | collective-permute-start | bytes 224 | tf_op jit(solution)/shard_map/ppermute | solution.py:650
  3.6 0.9 %copy-start = (bf16[3,3,3,32,32]{4,3,2,1,0:T(8,128)(2,1)S(1)}, bf16[3,3,3,32,32]{4,3,2,1,0:T(8,128)(2,1)}, u32[]{:S(2)}) copy-start(bf16[3,3,3,32,32]{4,3,2,1,0:T(8,128)(2,1)} %param.12) | copy-start | bytes 165892
  4.6 0.7 copy-start.1
  5.3 0.7 copy-start.2
  5.9 0.7 copy-start.3
  6.6 0.7 copy-start.4
  7.3 20.2 %copy-start.6 = (bf16[256,384]{1,0:T(8,128)(2,1)S(1)}, bf16[256,384]{1,0:T(8,128)(2,1)}, u32[]{:S(2)}) copy-start(bf16[256,384]{1,0:T(8,128)(2,1)} %constant.20.clone.refs_1_) | copy-start | bytes 589828
  7.3 20.2 %copy-start.7 = (f32[256,128]{1,0:T(8,128)S(1)}, f32[256,128]{1,0:T(8,128)}, u32[]{:S(2)}) copy-start(f32[256,128]{1,0:T(8,128)} %constant.21.clone.refs_5_) | copy-start | bytes 393220
  12.1 15.4 %collective-permute-start.1 = (bf16[4,4,16,256]{3,2,1,0:T(8,128)(2,1)S(1)}, bf16[4,4,16,256]{3,2,1,0:T(8,128)(2,1)S(1)}, u32[]{:S(2)}, u32[]{:S(2)}) collective-permute-start(bf16[4,4,16,256]{3,2,1,0:T(8,128)(2,1)S(1)} %get-tuple-element.40), channel_id=1, source_target_pairs={{1,0},{2,1},{3,2},{4,3},{5,4},{6,5},{7,6},{8,7},{9,8},{10,9},{11,1... | collective-permute-start | bytes 393224 | tf_op jit(solution)/shard_map/ppermute | solution.py:650
  18.2 9.3 %collective-permute-start.2 = (bf16[3,4,16,256]{3,2,1,0:T(8,128)(2,1)S(1)}, bf16[3,4,16,256]{3,2,1,0:T(8,128)(2,1)S(1)}, u32[]{:S(2)}, u32[]{:S(2)}) collective-permute-start(bf16[3,4,16,256]{3,2,1,0:T(8,128)(2,1)S(1)} %get-tuple-element.41), channel_id=1, source_target_pairs={{0,1},{1,2},{2,3},{3,0},{4,5},{5,6},{6,7},{7,4},{8,9},{9,10},{10,1... | collective-permute-start | bytes 294920 | tf_op jit(solution)/shard_map/ppermute | solution.py:655
  18.2 9.2 %collective-permute-start.3 = (bf16[3,4,16,256]{3,2,1,0:T(8,128)(2,1)S(1)}, bf16[3,4,16,256]{3,2,1,0:T(8,128)(2,1)S(1)}, u32[]{:S(2)}, u32[]{:S(2)}) collective-permute-start(bf16[3,4,16,256]{3,2,1,0:T(8,128)(2,1)S(1)} %get-tuple-element.42.here_ref), channel_id=1, source_target_pairs={{4,0},{8,4},{12,8},{16,12},{20,16},{24,20},{28,24},{32,28},{36,32}... | collective-permute-start | bytes 294920 | tf_op jit(solution)/shard_map/ppermute | solution.py:662
  20.2 7.3 %collective-permute-start.4 = (bf16[1,4,16,256]{3,2,1,0:T(8,128)(2,1)S(1)}, bf16[1,4,16,256]{3,2,1,0:T(8,128)(2,1)S(1)}, u32[]{:S(2)}, u32[]{:S(2)}) collective-permute-start(bf16[1,4,16,256]{3,2,1,0:T(8,128)(2,1)S(1)} %get-tuple-element.43), channel_id=1, source_target_pairs={{2,0},{3,1},{4,2},{5,3},{6,4},{7,5},{8,6},{9,7},{10,8},{11,9},{12,... | collective-permute-start | bytes 98312 | tf_op jit(solution)/shard_map/ppermute | solution.py:650
  27.5 36.4 %copy-start.5 = (bf16[256,4096]{1,0:T(8,128)(2,1)S(1)}, bf16[256,4096]{1,0:T(8,128)(2,1)}, u32[]{:S(2)}) copy-start(bf16[256,4096]{1,0:T(8,128)(2,1)} %constant.22.clone.parts_ref) | copy-start | bytes 6291460
  55.9 16.2 %collective-permute-start.6 = (bf16[4,4,32,256]{3,2,1,0:T(8,128)(2,1)S(1)}, bf16[4,4,32,256]{3,2,1,0:T(8,128)(2,1)S(1)}, u32[]{:S(2)}, u32[]{:S(2)}) collective-permute-start(bf16[4,4,32,256]{3,2,1,0:T(8,128)(2,1)S(1)} %get-tuple-element.54), channel_id=1, source_target_pairs={{0,1},{1,2},{2,3},{3,4},{4,5},{5,6},{6,7},{7,8},{8,9},{9,10},{10,1... | collective-permute-start | bytes 786440 | tf_op jit(solution)/shard_map/ppermute | solution.py:650
  57.8 14.3 %collective-permute-start.5 = (bf16[3,4,32,256]{3,2,1,0:T(8,128)(2,1)S(1)}, bf16[3,4,32,256]{3,2,1,0:T(8,128)(2,1)S(1)}, u32[]{:S(2)}, u32[]{:S(2)}) collective-permute-start(bf16[3,4,32,256]{3,2,1,0:T(8,128)(2,1)S(1)} %get-tuple-element.53), channel_id=1, source_target_pairs={{0,3},{1,0},{2,1},{3,2},{4,7},{5,4},{6,5},{7,6},{8,11},{9,8},{10,9... | collective-permute-start | bytes 589832 | tf_op jit(solution)/shard_map/ppermute | solution.py:655
  60.1 12.0 %collective-permute-start.7 = (bf16[3,4,32,256]{3,2,1,0:T(8,128)(2,1)S(1)}, bf16[3,4,32,256]{3,2,1,0:T(8,128)(2,1)S(1)}, u32[]{:S(2)}, u32[]{:S(2)}) collective-permute-start(bf16[3,4,32,256]{3,2,1,0:T(8,128)(2,1)S(1)} %get-tuple-element.55.here_ref), channel_id=1, source_target_pairs={{0,4},{4,8},{8,12},{12,16},{16,20},{20,24},{24,28},{28,32},{32,36}... | collective-permute-start | bytes 589832 | tf_op jit(solution)/shard_map/ppermute | solution.py:662
  62.0 10.1 %collective-permute-start.8 = (bf16[1,4,32,256]{3,2,1,0:T(8,128)(2,1)S(1)}, bf16[1,4,32,256]{3,2,1,0:T(8,128)(2,1)S(1)}, u32[]{:S(2)}, u32[]{:S(2)}) collective-permute-start(bf16[1,4,32,256]{3,2,1,0:T(8,128)(2,1)S(1)} %get-tuple-element.56), channel_id=1, source_target_pairs={{0,2},{1,3},{2,4},{3,5},{4,6},{5,7},{6,8},{7,9},{8,10},{9,11},{10,... | collective-permute-start | bytes 196616 | tf_op jit(solution)/shard_map/ppermute | solution.py:650
